TPU v7x, 32 devices: a whole 2x2x4 slice. The times are simulated.
32 devices in a mesh: col: 8 (over z, y), row: 4 (over x, core).
Axes of the slice: x: 2, y: 2, z: 4, core: 2. Of those that a mesh axis runs over, the one named last changes fastest.
Arguments:
- q_left: bfloat16 [4096, 4096], P('row'), may hold values from -2 to 2, as said below
- grad: bfloat16 [4096, 14336], P('row', 'col'), may hold values from -250 to 250
- q_right: float32 [14336], P('col'), may hold values from 0.5 to 2
Outputs:
- new_left: float32 [4096, 4096], P('row', 'col')
- precond: bfloat16 [4096, 14336], P('row', 'col')
Inputs may be any that keep to these rules, and one draw needn't show every extreme that they name: `q_left`: a diagonal of positive entries with dense off-diagonal entries.
All inputs are finite; a program needn't handle non-finite values.
Results may differ from a plain program's by a relative error of at most 0.0045.
Values may be sent and summed in bfloat16 or wider, within the bound.
A program may use at most 192 MiB of HBM per device.

v0:
```python
import jax
import jax.numpy as jnp
from jax import lax
from jax.sharding import PartitionSpec as P

step_rate = 0.5
epsilon = 1e-06


def shards(q_left, grad, q_right):
    rows_here = q_left.shape[0]
    order = q_left.shape[1]
    row_pos = lax.axis_index("row")
    col_pos = lax.axis_index("col")
    col_count = lax.axis_size("col")
    width = order // col_count
    left_cols = q_left
    acc = jnp.dot(
        left_cols,
        lax.all_gather(grad, "row", axis=0, tiled=True),
        preferred_element_type=jnp.float32,
    )
    act = (acc * q_right[None, :]).astype(jnp.bfloat16)
    act_panel = lax.all_gather(act, "row", axis=0, tiled=True)
    act_f = act.astype(jnp.float32)
    total_sq = lax.psum(jnp.sum(act_f * act_f), ("col", "row"))
    scale = total_sq / order + epsilon
    first_row = row_pos * rows_here
    q_mine = lax.dynamic_slice_in_dim(q_left, col_pos * width, width, 1)
    summed = lax.psum_scatter(
        lax.dot_general(
            act, act_panel, (((1,), (1,)), ((), ())), preferred_element_type=jnp.float32
        ),
        "col",
        scatter_dimension=0,
        tiled=True,
    )
    gram_panel = lax.all_gather(summed.astype(jnp.bfloat16), "col", axis=0, tiled=True)
    row_ids = first_row + lax.broadcasted_iota(jnp.int32, gram_panel.shape, 0)
    col_ids = lax.broadcasted_iota(jnp.int32, gram_panel.shape, 1)
    upper = jnp.where(col_ids >= row_ids, gram_panel, jnp.zeros_like(gram_panel))
    stepped = jnp.dot(
        upper, lax.all_gather(q_mine, "row", axis=0, tiled=True), preferred_element_type=jnp.float32
    )
    q_tile = q_mine.astype(jnp.float32)
    new_left = q_tile - step_rate * (stepped / scale - q_tile)
    left_cols = q_left
    pre = lax.psum_scatter(
        lax.dot_general(
            left_cols, act, (((0,), (0,)), ((), ())), preferred_element_type=jnp.float32
        ),
        "row",
        scatter_dimension=0,
        tiled=True,
    )
    precond = (pre * q_right[None, :]).astype(jnp.bfloat16)
    return (new_left, precond)


def solution(mesh):
    in_specs = (P("row", None), P("row", "col"), P("col"))
    out_specs = (P("row", "col"), P("row", "col"))
    return jax.shard_map(shards, mesh=mesh, in_specs=in_specs, out_specs=out_specs, check_vma=False)
```

profile of v0, /device:TPU:0, one launch (start us, length us, event | category | flops | bytes accessed | tf_op | source)
XLA Modules:
  0.0 918.3 jit_solution(14693187879836015015)
XLA Ops:
  7.2 0.0 all-gather.5.cloned.1.call-start
  7.2 0.7 all-gather.5.cloned.1.call-update
  7.9 0.0 all-gather.7.cloned.1.call-start
  7.9 98.4 %all-gather.5.cloned.1.call-done = bf16[4096,1792]{1,0:T(8,128)(2,1)} async-done(((bf16[1024,1792]{1,0:T(8,128)(2,1)}), bf16[4096,1792]{1,0:T(8,128)(2,1)}) %all-gather.5.cloned.1.call-update) | async-done | bytes 14680080 | tf_op jit(solution)/shard_map/all_gather | solution.py:20
  106.3 23.4 %multiply_reduce_fusion = (f32[]{:T(128)}, bf16[1024,1792]{1,0:T(8,128)(2,1)}) fusion(f32[1792]{0:T(1024)} %param.5, bf16[1024,4096]{1,0:T(8,128)(2,1)} %param.3, bf16[4096,1792]{1,0:T(8,128)(2,1)} %all-gather.5.cloned.1.call-done), kind=kOutput, calls=%fused_computation.6 | convolution fusion | flops 15041560576 | bytes 26745860 | tf_op jit(solution)/shard_map/dot_general | solution.py:18
  129.7 0.0 all-gather.7.cloned.1.call-update
  129.8 0.0 reduce-scatter.3.cloned.1.call-start
  129.8 94.1 %all-gather.7.cloned.1.call-done = bf16[4096,1792]{1,0:T(8,128)(2,1)} async-done(((bf16[1024,1792]{1,0:T(8,128)(2,1)}), bf16[4096,1792]{1,0:T(8,128)(2,1)}) %all-gather.7.cloned.1.call-update) | async-done | bytes 14680080 | tf_op jit(solution)/shard_map/all_gather | solution.py:24
  223.9 21.1 %fusion.9 = f32[1024,4096]{1,0:T(8,128)} fusion(bf16[1024,1792]{1,0:T(8,128)(2,1)} %get-tuple-element.3, bf16[4096,1792]{1,0:T(8,128)(2,1)} %all-gather.7.cloned.1.call-done), kind=kOutput, calls=%fused_computation.15 | convolution fusion | flops 15032385536 | bytes 35127296 | tf_op jit(solution)/shard_map/dot_general | solution.py:31
  245.1 0.0 reduce-scatter.3.cloned.1.call-update
  245.1 0.0 reduce-scatter.5.cloned.1.call-start
  245.1 22.8 %convolution_bitcast_fusion = f32[4096,1792]{1,0:T(8,128)} fusion(bf16[1024,1792]{1,0:T(8,128)(2,1)} %get-tuple-element.3, bf16[1024,4096]{1,0:T(8,128)(2,1)} %param.3), kind=kOutput, calls=%fused_computation | convolution fusion | flops 15032385536 | bytes 41418752 | tf_op jit(solution)/shard_map/dot_general | solution.py:49
  267.9 0.0 reduce-scatter.5.cloned.1.call-update
  268.0 0.0 copy-start.1
  268.0 0.0 all-gather.11.cloned.1.call-start
  268.0 2.3 constant_dynamic-slice_fusion
  270.3 0.0 all-gather.11.cloned.1.call-update
  270.3 0.0 copy-start
  270.4 0.0 all-gather.9.cloned.1.call-start
  270.4 257.5 %reduce-scatter.3.cloned.1.call-done = f32[128,4096]{1,0:T(8,128)} async-done(((f32[1024,4096]{1,0:T(8,128)}), f32[128,4096]{1,0:T(8,128)}) %reduce-scatter.3.cloned.1.call-update) | async-done | bytes 2097168 | tf_op jit(solution)/shard_map/reduce_scatter | solution.py:30
  527.9 2.7 convert_element_type.17
  530.6 0.0 all-gather.9.cloned.1.call-update
  530.6 39.4 %psum.7 = f32[]{:T(128)} all-reduce(f32[]{:T(128)} %get-tuple-element.2), channel_id=1, replica_groups=mesh['col'=8,'row'=4] {'col','row'}, use_global_device_ids=true, to_apply=%region_2.0 | all-reduce | flops 1 | bytes 8 | tf_op jit(solution)/shard_map/psum | solution.py:26
  570.6 166.8 %reduce-scatter.5.cloned.1.call-done = f32[1024,1792]{1,0:T(8,128)} async-done(((f32[4096,1792]{1,0:T(8,128)}), f32[1024,1792]{1,0:T(8,128)}) %reduce-scatter.5.cloned.1.call-update) | async-done | bytes 7340048 | tf_op jit(solution)/shard_map/reduce_scatter | solution.py:48
  737.4 0.0 copy-done.1
  737.4 5.5 multiply_convert_fusion
  742.9 31.0 %all-gather.11.cloned.1.call-done = bf16[4096,512]{1,0:T(8,128)(2,1)} async-done(((bf16[1024,512]{1,0:T(8,128)(2,1)}), bf16[4096,512]{1,0:T(8,128)(2,1)}) %all-gather.11.cloned.1.call-update) | async-done | bytes 4194320 | tf_op jit(solution)/shard_map/all_gather | solution.py:43
  773.9 127.0 %all-gather.9.cloned.1.call-done = bf16[1024,4096]{1,0:T(8,128)(2,1)} async-done(((bf16[128,4096]{1,0:T(8,128)(2,1)}), bf16[1024,4096]{1,0:T(8,128)(2,1)}) %all-gather.9.cloned.1.call-update) | async-done | bytes 8388624 | tf_op jit(solution)/shard_map/all_gather | solution.py:38
  900.9 0.0 copy-done
  900.9 10.6 %convert_subtract_fusion = f32[1024,512]{1,0:T(8,128)} fusion(bf16[1024,512]{1,0:T(8,128)(2,1)S(1)} %copy-done, f32[]{:T(128)S(6)} %add.22, bf16[4096,512]{1,0:T(8,128)(2,1)} %all-gather.11.cloned.1.call-done, bf16[1024,4096]{1,0:T(8,128)(2,1)} %all-gather.9.cloned.1.call-done, s32[1024]{0:T(1024)S(1)} %iota_add_fusion), kind=kOutput, calls=%fused_computation.9 | convolution fusion | flops 4305977344 | bytes 15732740 | tf_op jit(solution)/shard_map/dot_general | solution.py:42
  (1 shorter events, 0.0 us)
Async XLA Ops:
  7.2 99.1 %all-gather.5.cloned.1.call-start = ((), (), s32[]{:S(2)}) async-start(), calls=%async_computation.2 | async-start | bytes 18350080 | tf_op jit(solution)/shard_map/all_gather | solution.py:20
  7.9 216.0 %all-gather.7.cloned.1.call-start = ((), (), s32[]{:S(2)}) async-start(), calls=%async_computation.3 | async-start | bytes 18350080 | tf_op jit(solution)/shard_map/all_gather | solution.py:24
  129.8 398.1 %reduce-scatter.3.cloned.1.call-start = ((), (), s32[]{:S(2)}) async-start(), calls=%async_computation.4 | async-start | bytes 18874368 | tf_op jit(solution)/shard_map/reduce_scatter | solution.py:30
  245.1 492.3 %reduce-scatter.5.cloned.1.call-start = ((), (), s32[]{:S(2)}) async-start(), calls=%async_computation.7 | async-start | bytes 36700160 | tf_op jit(solution)/shard_map/reduce_scatter | solution.py:48
  268.0 469.5 %copy-start.1 = (f32[1792]{0:T(1024)S(1)}, f32[1792]{0:T(1024)}, u32[]{:S(2)}) copy-start(f32[1792]{0:T(1024)} %param.5) | copy-start | bytes 21508
  268.0 506.0 %all-gather.11.cloned.1.call-start = ((), (), s32[]{:S(2)}) async-start(), calls=%async_computation.6 | async-start | bytes 5242880 | tf_op jit(solution)/shard_map/all_gather | solution.py:43
  270.3 630.5 %copy-start = (bf16[1024,512]{1,0:T(8,128)(2,1)S(1)}, bf16[1024,512]{1,0:T(8,128)(2,1)}, u32[]{:S(2)}) copy-start(bf16[1024,512]{1,0:T(8,128)(2,1)} %constant_dynamic-slice_fusion) | copy-start | bytes 3145732
  270.4 630.5 %all-gather.9.cloned.1.call-start = ((), (), s32[]{:S(2)}) async-start(), calls=%async_computation.5 | async-start | bytes 9437184 | tf_op jit(solution)/shard_map/all_gather | solution.py:38
Sparse Core Ops, SparseCore 0:
  9.6 96.6 all-gather.4
  129.9 94.0 all-gather.6
  245.2 282.6 reduce-scatter.2
  530.5 206.8 reduce-scatter.4
  739.4 34.4 all-gather.10
  775.9 124.9 all-gather.8
where the time goes:
time: 919 us; the launch traced here: 918 us
  waiting for transfers between devices  775 us (84%)
  matrix products  77.9 us (8%)
  blocking collectives  39.4 us (4%)
  between operations  14.8 us (2%)
    reduce_scatter x1, waiting for transfers between devices, shards(): lax.psum_scatter(lax.dot_general(act, act_panel, (((1,), (1,)), ((), ()))...  257 us
    reduce_scatter x1, waiting for transfers between devices, shards(): lax.psum_scatter(lax.dot_general(left_cols, act, (((0,), (0,)), ((), ()))...  167 us
    all_gather x1, waiting for transfers between devices, shards(): lax.all_gather(summed.astype(jnp.bfloat16), 'col', axis=0, tiled=True)  127 us
    all_gather x1, waiting for transfers between devices, shards(): lax.all_gather(grad, 'row', axis=0, tiled=True)  98.4 us
    all_gather x1, waiting for transfers between devices, shards(): act_panel = lax.all_gather(act, 'row', axis=0, tiled=True)  94.1 us
    psum x1, blocking collectives, shards(): total_sq = lax.psum(jnp.sum(act_f * act_f), ('col', 'row'))  39.4 us
    all_gather x1, waiting for transfers between devices, shards(): lax.all_gather(q_mine, 'row', axis=0, tiled=True)  31 us
    dot_general x1, matrix products, shards(): jnp.dot(left_cols, lax.all_gather(grad, 'row', axis=0, tiled=True), prefe...  23.4 us
  transfers between devices with their start and end apart: 6, of which 6 were waited for; matrix products, arithmetic and copies ran while one was open for 4% of the time, Pallas kernels for 0%

commit v1 on v0

v1 whole, which is shorter than its diff:
```python
import jax
import jax.numpy as jnp
from jax import lax
from jax.sharding import PartitionSpec as P

step_rate = 0.5
epsilon = 1e-06
f32 = jnp.float32
bf16 = jnp.bfloat16


def dot_nn(a, b):
    return lax.dot_general(a, b, (((1,), (0,)), ((), ())), preferred_element_type=f32)


def dot_nt(a, b):
    return lax.dot_general(a, b, (((1,), (1,)), ((), ())), preferred_element_type=f32)


def dot_tn(a, b):
    return lax.dot_general(a, b, (((0,), (0,)), ((), ())), preferred_element_type=f32)


def swap(x, by):
    return lax.ppermute(x, "row", [(i, i ^ by) for i in range(4)])


def shards(q_left, grad, q_right):
    rows, order = q_left.shape
    r = lax.axis_index("row")
    c = lax.axis_index("col")
    col_count = lax.axis_size("col")
    assert lax.axis_size("row") == 4
    piece = rows // col_count
    width = order // col_count
    half = rows // 2

    grad_all = lax.all_gather(grad, "row", axis=0, tiled=True)
    q_far_piece = swap(lax.dynamic_slice_in_dim(q_left, c * piece, piece, 0), 2)
    q_far = lax.all_gather(q_far_piece, "col", axis=0, tiled=True)
    q_mate = swap(q_left, 1)
    q_far_mate = swap(q_far, 1)

    def act_of(q):
        return (dot_nn(q, grad_all) * q_right[None, :]).astype(bf16)

    own = act_of(q_left)
    far = act_of(q_far)
    mate = swap(own, 1)
    far_mate = swap(far, 1)

    own_f = own.astype(f32)
    total_sq = lax.psum(jnp.sum(own_f * own_f), ("col", "row"))
    scale = total_sq / order + epsilon

    even = (r % 2) == 0
    lhs2 = jnp.where(r == 3, far_mate, own)
    rhs2 = jnp.where(even, mate, jnp.where(r == 3, own, far_mate))
    lhs3 = jnp.where(r >= 2, far, own)
    rhs3 = jnp.where(r >= 2, own[half:], far[:half])
    part = jnp.concatenate(
        [dot_nt(own, own).astype(bf16), dot_nt(lhs2, rhs2).astype(bf16), dot_nt(lhs3, rhs3).astype(bf16)],
        axis=1,
    )
    gram = lax.psum_scatter(part, "col", scatter_dimension=0, tiled=True)
    p1 = gram[:, :rows]
    p2 = gram[:, rows : 2 * rows]
    p3 = gram[:, 2 * rows :]
    got2 = lax.ppermute(p2, "row", [(3, 0)])
    got3 = lax.ppermute(p3, "row", [(2, 0), (3, 1)])
    zero = jnp.zeros_like(p1)
    row_ids = c * piece + lax.broadcasted_iota(jnp.int32, p1.shape, 0)
    col_ids = lax.broadcasted_iota(jnp.int32, p1.shape, 1)
    upper = jnp.concatenate(
        [
            jnp.where(col_ids >= row_ids, p1, zero),
            jnp.where(even, p2, zero),
            jnp.where(r < 2, jnp.concatenate([p3, got3], axis=1), zero),
            jnp.where(r == 0, got2, jnp.where(r == 1, p2, zero)),
        ],
        axis=1,
    )
    q_all = jnp.concatenate([q_left, q_mate, q_far, q_far_mate], axis=0)
    ratio = (dot_nn(upper, q_all) / scale).astype(bf16)
    ratio = lax.all_to_all(ratio, "col", split_axis=1, concat_axis=0, tiled=True)
    q_tile = lax.dynamic_slice_in_dim(q_left, c * width, width, 1).astype(f32)
    new_left = q_tile - step_rate * (ratio.astype(f32) - q_tile)

    q_cols = lax.dynamic_slice_in_dim(q_all, r * rows, rows, 1)
    act_all = jnp.concatenate([own, mate, far, far_mate], axis=0)
    precond = (dot_tn(q_cols, act_all) * q_right[None, :]).astype(bf16)
    return (new_left, precond)


def solution(mesh):
    in_specs = (P("row", None), P("row", "col"), P("col"))
    out_specs = (P("row", "col"), P("row", "col"))
    return jax.shard_map(shards, mesh=mesh, in_specs=in_specs, out_specs=out_specs, check_vma=False)
```

time: 919 us -> 478 us (0.52)
  waiting for transfers between devices: 775 us -> 245 us
  local copies, waits for them, and re-layouts: 2.3 us -> 44.4 us
  matrix products: 77.9 us -> 108 us
  starting transfers between devices: 0.24 us -> 10.9 us
    reduce_scatter x2 -> x0, waiting for transfers between devices: 424 us -> none  [the longest x1 257 us: shards(): lax.psum_scatter(lax.dot_general(act, act_panel, (((1,), (1,)), ((), ()))...]
    all_gather x4 -> x2, waiting for transfers between devices: 350 us -> 174 us  [the longest x1 105 us: shards(): q_far = lax.all_gather(q_far_piece, 'col', axis=0, tiled=True)]
    ppermute x0 -> x7, waiting for transfers between devices: none -> 46.6 us  [the longest x5 40 us: swap(): return lax.ppermute(x, 'row', [(i, i ^ by) for i in range(4)])]
    unnamed x4 -> x11, local copies, waits for them, and re-layouts: 0.01 us -> 32.3 us
    dot_general x4 -> x7, matrix products: 77.9 us -> 108 us  [the longest x3 61.1 us: dot_nn(): lax.dot_general(a, b, (((1,), (0,)), ((), ())), preferred_element_type=f32)]
    unnamed x6 -> x4, waiting for transfers between devices: 0.76 us -> 25.2 us
    concatenate x0 -> x1, other arithmetic: none -> 11.2 us  [shards(): jnp.concatenate([dot_nt(own, own).astype(bf16), dot_nt(lhs2, rhs2).astype...]
  transfers between devices with their start and end apart: 6 -> 11, of which waited for: 6 -> 6; matrix products, arithmetic and copies ran while one was open for 4% -> 25% of each run, Pallas kernels for 0% -> 0%
where the time goes in v1:
time: 478 us
  waiting for transfers between devices  245 us (51%)
  matrix products  108 us (23%)
  local copies, waits for them, and re-layouts  44.4 us (9%)
  blocking collectives  40 us (8%)
  between operations  14.6 us (3%)
  other arithmetic  14.3 us (3%)
  starting transfers between devices  10.9 us (2%)
    all_gather x1, waiting for transfers between devices, shards(): q_far = lax.all_gather(q_far_piece, 'col', axis=0, tiled=True)  105 us
    all_gather x1, waiting for transfers between devices, shards(): grad_all = lax.all_gather(grad, 'row', axis=0, tiled=True)  68.1 us
    dot_general x3, matrix products, dot_nn(): lax.dot_general(a, b, (((1,), (0,)), ((), ())), preferred_element_type=f32)  61.1 us
    ppermute x5, waiting for transfers between devices, swap(): return lax.ppermute(x, 'row', [(i, i ^ by) for i in range(4)])  40 us
    psum x1, blocking collectives, shards(): total_sq = lax.psum(jnp.sum(own_f * own_f), ('col', 'row'))  40 us
    unnamed x11, local copies, waits for them, and re-layouts  32.3 us
    dot_general x1, matrix products, dot_tn(): lax.dot_general(a, b, (((0,), (0,)), ((), ())), preferred_element_type=f32)  26.6 us
    unnamed x4, waiting for transfers between devices  25.2 us
  transfers between devices with their start and end apart: 11, of which 6 were waited for; matrix products, arithmetic and copies ran while one was open for 25% of the time, Pallas kernels for 0%

profile of v1, /device:TPU:0, one launch (start us, length us, event | category | flops | bytes accessed | tf_op | source)
XLA Modules:
  0.0 477.8 jit_solution(13971047880663855013)
XLA Ops:
  7.2 0.7 all-gather.3.cloned.1.call-update
  8.0 1.3 constant_dynamic-slice_fusion
  9.3 3.0 collective-permute-start
  12.3 34.7 %collective-permute-done = bf16[128,4096]{1,0:T(8,128)(2,1)S(1)} collective-permute-done((bf16[128,4096]{1,0:T(8,128)(2,1)S(1)}, bf16[128,4096]{1,0:T(8,128)(2,1)S(1)}, u32[]{:S(2)}, u32[]{:S(2)}) %collective-permute-start) | collective-permute-done | bytes 1048608 | tf_op jit(solution)/shard_map/ppermute | solution.py:25
  47.0 1.0 copy-done
  48.0 68.1 %all-gather.3.cloned.1.call-done = bf16[4096,1792]{1,0:T(8,128)(2,1)} async-done(((bf16[1024,1792]{1,0:T(8,128)(2,1)}), bf16[4096,1792]{1,0:T(8,128)(2,1)}) %all-gather.3.cloned.1.call-update) | async-done | bytes 14680080 | tf_op jit(solution)/shard_map/all_gather | solution.py:38
  116.1 23.4 %multiply_reduce_fusion = (f32[]{:T(128)}, bf16[1024,1792]{1,0:T(8,128)(2,1)}) fusion(f32[1792]{0:T(1024)S(1)} %copy-done.1, bf16[1024,4096]{1,0:T(8,128)(2,1)} %param.3, bf16[4096,1792]{1,0:T(8,128)(2,1)} %all-gather.3.cloned.1.call-done), kind=kOutput, calls=%fused_computation.10 | convolution fusion | flops 15041560576 | bytes 26745860 | tf_op jit(solution)/shard_map/dot_general | solution.py:13
  139.8 105.5 %all-gather.5.cloned.1.call-done = bf16[1024,4096]{1,0:T(8,128)(2,1)} async-done(((bf16[128,4096]{1,0:T(8,128)(2,1)}), bf16[1024,4096]{1,0:T(8,128)(2,1)}) %all-gather.5.cloned.1.call-update) | async-done | bytes 8388624 | tf_op jit(solution)/shard_map/all_gather | solution.py:40
  245.2 22.6 %multiply_convert_fusion.1 = bf16[1024,1792]{1,0:T(8,128)(2,1)} fusion(bf16[1024,4096]{1,0:T(8,128)(2,1)} %all-gather.5.cloned.1.call-done, bf16[4096,1792]{1,0:T(8,128)(2,1)} %all-gather.3.cloned.1.call-done, f32[1792]{0:T(1024)S(1)} %copy-done.1), kind=kOutput, calls=%fused_computation.11 | convolution fusion | flops 15036055552 | bytes 26745856 | tf_op jit(solution)/shard_map/dot_general | solution.py:13
  267.9 5.3 %fusion.31 = bf16[1024,512]{0,1:T(8,128)(2,1)S(1)} fusion(bf16[1024,1792]{1,0:T(8,128)(2,1)} %multiply_convert_fusion.1, bf16[1024,1792]{1,0:T(8,128)(2,1)} %get-tuple-element.7, pred[]{:T(512)S(6)} %ge.8), kind=kOutput, calls=%fused_computation.33 | convolution fusion | flops 1882324992 | bytes 12059648 | tf_op jit(solution)/shard_map/dot_general | solution.py:17
  273.1 7.1 %convolution_convert_fusion = bf16[1024,1024]{0,1:T(8,128)(2,1)S(1)} fusion(bf16[1024,1792]{1,0:T(8,128)(2,1)} %get-tuple-element.7), kind=kOutput, calls=%fused_computation.29 | convolution fusion | flops 3759144960 | bytes 5767168 | tf_op jit(solution)/shard_map/dot_general | solution.py:17
  280.3 8.2 %fusion.24 = bf16[1024,1024]{0,1:T(8,128)(2,1)S(1)} fusion(bf16[1024,1792]{1,0:T(8,128)(2,1)} %collective-permute-done.2, bf16[1024,1792]{1,0:T(8,128)(2,1)} %get-tuple-element.7, bf16[1024,1792]{1,0:T(8,128)(2,1)} %collective-permute-done.1, pred[]{:T(512)S(6)} %eq.16, pred[]{:T(512)S(6)} %eq.15), kind=kOutput, calls=%fused_computation.28 | convolution fusion | flops 3764649984 | bytes 13107202 | tf_op jit(solution)/shard_map/dot_general | solution.py:17
  288.5 11.2 %pad_maximum_fusion = bf16[1024,2560]{0,1:T(8,128)(2,1)} fusion(bf16[1024,512]{0,1:T(8,128)(2,1)S(1)} %fusion.31, bf16[1024,1024]{0,1:T(8,128)(2,1)S(1)} %fusion.24, bf16[1024,1024]{0,1:T(8,128)(2,1)S(1)} %convolution_convert_fusion), kind=kLoop, calls=%fused_computation.13 | loop fusion | flops 15728640 | bytes 10485760 | tf_op jit(solution)/shard_map/concatenate | solution.py:61
  299.7 7.7 %copy.7 = bf16[1024,2560]{1,0:T(8,128)(2,1)} copy(bf16[1024,2560]{0,1:T(8,128)(2,1)} %pad_maximum_fusion) | data formatting | bytes 10485760
  307.5 0.5 collective-permute-start.6
  308.0 7.7 %constant_dynamic-update-slice_fusion.3 = bf16[4096,4096]{1,0:T(8,128)(2,1)} fusion(bf16[1024,4096]{1,0:T(8,128)(2,1)} %param.3), kind=kLoop, calls=%fused_computation.50 | loop fusion | bytes 16777216
  315.7 5.3 %collective-permute-done.5 = bf16[1024,4096]{1,0:T(8,128)(2,1)} collective-permute-done((bf16[1024,4096]{1,0:T(8,128)(2,1)}, bf16[1024,4096]{1,0:T(8,128)(2,1)}, u32[]{:S(2)}, u32[]{:S(2)}) %collective-permute-start.5) | collective-permute-done | bytes 8388640 | tf_op jit(solution)/shard_map/ppermute | solution.py:25
  321.0 7.8 %constant_dynamic-update-slice_fusion.2 = bf16[4096,4096]{1,0:T(8,128)(2,1)} fusion(bf16[4096,4096]{1,0:T(8,128)(2,1)} %constant_dynamic-update-slice_fusion.3, bf16[1024,4096]{1,0:T(8,128)(2,1)} %collective-permute-done.5), kind=kLoop, calls=%fused_computation.49 | loop fusion | bytes 16777216
  328.7 7.8 %constant_dynamic-update-slice_fusion.1 = bf16[4096,4096]{1,0:T(8,128)(2,1)} fusion(bf16[4096,4096]{1,0:T(8,128)(2,1)} %constant_dynamic-update-slice_fusion.2, bf16[1024,4096]{1,0:T(8,128)(2,1)} %all-gather.5.cloned.1.call-done), kind=kLoop, calls=%fused_computation.48 | loop fusion | bytes 16777216
  336.5 40.0 %psum.7 = f32[]{:T(128)} all-reduce(f32[]{:T(128)} %get-tuple-element.6), channel_id=1, replica_groups=mesh['col'=8,'row'=4] {'col','row'}, use_global_device_ids=true, to_apply=%region_2.3 | all-reduce | flops 1 | bytes 8 | tf_op jit(solution)/shard_map/psum | solution.py:53
  377.2 7.7 %constant_dynamic-update-slice_fusion = bf16[4096,4096]{1,0:T(8,128)(2,1)} fusion(bf16[4096,4096]{1,0:T(8,128)(2,1)} %constant_dynamic-update-slice_fusion.1, bf16[1024,4096]{1,0:T(8,128)(2,1)} %collective-permute-done.6), kind=kLoop, calls=%fused_computation.47 | loop fusion | bytes 16777216 | tf_op jit(solution)/shard_map/concatenate | solution.py:83
  384.9 24.5 %reduce-scatter.4.cloned.1.call-done = bf16[128,2560]{1,0:T(8,128)(2,1)} async-done(((bf16[1024,2560]{1,0:T(8,128)(2,1)}), bf16[128,2560]{1,0:T(8,128)(2,1)}) %reduce-scatter.4.cloned.1.call-update) | async-done | bytes 655376
  409.4 1.1 fusion.45
  410.6 1.3 collective-permute-start.4
  411.9 0.9 slice.24
  412.9 1.3 collective-permute-start.3
  414.5 6.6 %collective-permute-done.3 = bf16[128,512]{0,1:T(8,128)(2,1)S(1)} collective-permute-done((bf16[128,512]{0,1:T(8,128)(2,1)S(1)}, bf16[128,512]{0,1:T(8,128)(2,1)S(1)}, u32[]{:S(2)}, u32[]{:S(2)}) %collective-permute-start.3) | collective-permute-done | bytes 131104 | tf_op jit(solution)/shard_map/ppermute | solution.py:70
  421.2 15.1 %fusion.9 = bf16[128,4096]{1,0:T(8,128)(2,1)S(1)} fusion(bf16[4096,4096]{1,0:T(8,128)(2,1)} %constant_dynamic-update-slice_fusion, bf16[128,1024]{0,1:T(8,128)(2,1)S(1)} %get-tuple-element.5, bf16[128,1024]{0,1:T(8,128)(2,1)S(1)} %maximum_select_fusion, bf16[128,1024]{0,1:T(8,128)(2,1)S(1)} %get-tuple-element.4, bf16[128,1024]{0,1:T(8,128)(2,1)S(1)} %fusion.41, ...), kind=kOutput, calls=%fused_computation.15 | convolution fusion | flops 4300210176 | bytes 35651588 | tf_op jit(solution)/shard_map/dot_general | solution.py:13
  436.3 1.1 copy.14
  437.4 4.4 all-to-all-start
  441.8 26.6 %multiply_convert_fusion = bf16[1024,1792]{1,0:T(8,128)(2,1)} fusion(f32[1792]{0:T(1024)S(1)} %copy-done.1, bf16[1024,1792]{1,0:T(8,128)(2,1)} %collective-permute-done.1, bf16[1024,1792]{1,0:T(8,128)(2,1)} %multiply_convert_fusion.1, bf16[1024,1792]{1,0:T(8,128)(2,1)} %collective-permute-done.2, bf16[1024,1792]{1,0:T(8,128)(2,1)} %get-tuple-element.7, ...), kind=kOutput, calls=%fused_computation.9 | convolution fusion | flops 15094775808 | bytes 26745860 | tf_op jit(solution)/shard_map/dot_general | solution.py:21
  468.3 2.9 convert_subtract_fusion
  (23 shorter events, 1.1 us)
Async XLA Ops:
  7.2 109.0 %copy-start.1 = (f32[1792]{0:T(1024)S(1)}, f32[1792]{0:T(1024)}, u32[]{:S(2)}) copy-start(f32[1792]{0:T(1024)} %param.5) | copy-start | bytes 21508
  7.2 109.0 %all-gather.3.cloned.1.call-start = ((), (), s32[]{:S(2)}) async-start(), calls=%async_computation.2 | async-start | bytes 18350080 | tf_op jit(solution)/shard_map/all_gather | solution.py:38
  7.9 237.3 %all-gather.5.cloned.1.call-start = ((), (), s32[]{:S(2)}) async-start(), calls=%async_computation.3 | async-start | bytes 9437184 | tf_op jit(solution)/shard_map/all_gather | solution.py:40
  9.3 37.7 %collective-permute-start = (bf16[128,4096]{1,0:T(8,128)(2,1)S(1)}, bf16[128,4096]{1,0:T(8,128)(2,1)S(1)}, u32[]{:S(2)}, u32[]{:S(2)}) collective-permute-start(bf16[128,4096]{1,0:T(8,128)(2,1)S(1)} %constant_dynamic-slice_fusion), channel_id=1, source_target_pairs={{0,2},{1,3},{2,0},{3,1},{4,6},{5,7},{6,4},{7,5},{8,10},{9,11},{10,... | collective-permute-start | bytes 3145736 | tf_op jit(solution)/shard_map/ppermute | solution.py:25
  46.9 1.0 copy-start
  47.9 361.4 %reduce-scatter.4.cloned.1.call-start = ((), (), s32[]{:S(2)}) async-start(), calls=%async_computation.4 | async-start | bytes 5898240
  139.5 140.7 %collective-permute-start.2 = (bf16[1024,1792]{1,0:T(8,128)(2,1)}, bf16[1024,1792]{1,0:T(8,128)(2,1)}, u32[]{:S(2)}, u32[]{:S(2)}) collective-permute-start(bf16[1024,1792]{1,0:T(8,128)(2,1)} %get-tuple-element.7), channel_id=1, source_target_pairs={{0,1},{1,0},{2,3},{3,2},{4,5},{5,4},{6,7},{7,6},{8,9},{9,8},{10,11... | collective-permute-start | bytes 11010056 | tf_op jit(solution)/shard_map/ppermute | solution.py:25
  267.8 12.4 %collective-permute-start.1 = (bf16[1024,1792]{1,0:T(8,128)(2,1)}, bf16[1024,1792]{1,0:T(8,128)(2,1)}, u32[]{:S(2)}, u32[]{:S(2)}) collective-permute-start(bf16[1024,1792]{1,0:T(8,128)(2,1)} %multiply_convert_fusion.1), channel_id=1, source_target_pairs={{0,1},{1,0},{2,3},{3,2},{4,5},{5,4},{6,7},{7,6},{8,9},{9,8},{10,11... | collective-permute-start | bytes 11010056 | tf_op jit(solution)/shard_map/ppermute | solution.py:25
  307.4 13.6 %collective-permute-start.5 = (bf16[1024,4096]{1,0:T(8,128)(2,1)}, bf16[1024,4096]{1,0:T(8,128)(2,1)}, u32[]{:S(2)}, u32[]{:S(2)}) collective-permute-start(bf16[1024,4096]{1,0:T(8,128)(2,1)} %param.3), channel_id=1, source_target_pairs={{0,1},{1,0},{2,3},{3,2},{4,5},{5,4},{6,7},{7,6},{8,9},{9,8},{10,11... | collective-permute-start | bytes 25165832 | tf_op jit(solution)/shard_map/ppermute | solution.py:25
  307.5 69.7 %collective-permute-start.6 = (bf16[1024,4096]{1,0:T(8,128)(2,1)}, bf16[1024,4096]{1,0:T(8,128)(2,1)}, u32[]{:S(2)}, u32[]{:S(2)}) collective-permute-start(bf16[1024,4096]{1,0:T(8,128)(2,1)} %all-gather.5.cloned.1.call-done), channel_id=1, source_target_pairs={{0,1},{1,0},{2,3},{3,2},{4,5},{5,4},{6,7},{7,6},{8,9},{9,8},{10,11... | collective-permute-start | bytes 25165832 | tf_op jit(solution)/shard_map/ppermute | solution.py:25
  410.6 10.6 %collective-permute-start.4 = (bf16[128,1024]{0,1:T(8,128)(2,1)S(1)}, bf16[128,1024]{0,1:T(8,128)(2,1)S(1)}, u32[]{:S(2)}, u32[]{:S(2)}) collective-permute-start(bf16[128,1024]{0,1:T(8,128)(2,1)S(1)} %copy.10), channel_id=1, source_target_pairs={{3,0},{7,4},{11,8},{15,12},{19,16},{23,20},{27,24},{31,28}} | collective-permute-start | bytes 786440 | tf_op jit(solution)/shard_map/ppermute | solution.py:69
  412.9 8.2 %collective-permute-start.3 = (bf16[128,512]{0,1:T(8,128)(2,1)S(1)}, bf16[128,512]{0,1:T(8,128)(2,1)S(1)}, u32[]{:S(2)}, u32[]{:S(2)}) collective-permute-start(bf16[128,512]{0,1:T(8,128)(2,1)S(1)} %copy.11), channel_id=1, source_target_pairs={{2,0},{3,1},{6,4},{7,5},{10,8},{11,9},{14,12},{15,13},{18,16},{19,... | collective-permute-start | bytes 393224 | tf_op jit(solution)/shard_map/ppermute | solution.py:70
  437.4 30.9 %all-to-all-start = ((bf16[128,8,512]{2,0,1:T(8,128)(2,1)}), bf16[128,8,512]{2,0,1:T(8,128)(2,1)S(1)}, u32[]{:S(2)}, u32[]{:S(2)}) async-start(bf16[128,8,512]{2,0,1:T(8,128)(2,1)} %bitcast.15), calls=%async_computation | async-start | bytes 2097152 | tf_op jit(solution)/shard_map/all_to_all | solution.py:85
Sparse Core Ops, SparseCore 0:
  9.6 106.5 all-gather.2
  118.8 126.3 all-gather.4
  307.5 101.7 reduce-scatter.3

commit v2 on v1

--- a/solution.py
+++ b/solution.py
@@ -35,39 +35,67 @@
     width = order // col_count
     half = rows // 2
 
-    grad_all = lax.all_gather(grad, "row", axis=0, tiled=True)
-    q_far_piece = swap(lax.dynamic_slice_in_dim(q_left, c * piece, piece, 0), 2)
-    q_far = lax.all_gather(q_far_piece, "col", axis=0, tiled=True)
+    def far_half(p):
+        mine = lax.dynamic_slice_in_dim(q_left, p * half + c * (piece // 2), piece // 2, 0)
+        return lax.all_gather(swap(mine, 2), "col", axis=0, tiled=True)
+
+    q_far0 = far_half(0)
+    q_far1 = far_half(1)
+    grad_far = swap(grad, 2)
+    grad_mate = swap(grad, 1)
+    grad_far_mate = swap(grad_far, 1)
+    grad_all = jnp.zeros((order,) + grad.shape[1:], grad.dtype)
+    for by, block in ((0, grad), (1, grad_mate), (2, grad_far), (3, grad_far_mate)):
+        grad_all = lax.dynamic_update_slice_in_dim(grad_all, block, (r ^ by) * rows, 0)
     q_mate = swap(q_left, 1)
-    q_far_mate = swap(q_far, 1)
+    q_far_mate0 = swap(q_far0, 1)
+    q_far_mate1 = swap(q_far1, 1)
 
     def act_of(q):
         return (dot_nn(q, grad_all) * q_right[None, :]).astype(bf16)
 
     own = act_of(q_left)
-    far = act_of(q_far)
     mate = swap(own, 1)
-    far_mate = swap(far, 1)
+    far0 = act_of(q_far0)
+    far_mate0 = swap(far0, 1)
+    far1 = act_of(q_far1)
+    far_mate1 = swap(far1, 1)
+    far = jnp.concatenate([far0, far1], axis=0)
+    far_mate = jnp.concatenate([far_mate0, far_mate1], axis=0)
 
     own_f = own.astype(f32)
-    total_sq = lax.psum(jnp.sum(own_f * own_f), ("col", "row"))
+    total_sq = jnp.sum(own_f * own_f).reshape(1, 1)
+    total_sq = total_sq + swap(total_sq, 1)
+    total_sq = total_sq + swap(total_sq, 2)
+    by = 1
+    while by < col_count:
+        total_sq = total_sq + lax.ppermute(total_sq, "col", [(i, i ^ by) for i in range(col_count)])
+        by *= 2
     scale = total_sq / order + epsilon
 
     even = (r % 2) == 0
     lhs2 = jnp.where(r == 3, far_mate, own)
     rhs2 = jnp.where(even, mate, jnp.where(r == 3, own, far_mate))
     lhs3 = jnp.where(r >= 2, far, own)
-    rhs3 = jnp.where(r >= 2, own[half:], far[:half])
-    part = jnp.concatenate(
-        [dot_nt(own, own).astype(bf16), dot_nt(lhs2, rhs2).astype(bf16), dot_nt(lhs3, rhs3).astype(bf16)],
-        axis=1,
+    rhs3 = jnp.where(r >= 2, own[half:], far0)
+
+    def col_sum(a, b):
+        return lax.psum_scatter(dot_nt(a, b).astype(bf16), "col", scatter_dimension=0, tiled=True)
+
+    p1 = col_sum(own, own)
+    p3 = col_sum(lhs3, rhs3)
+    p2 = col_sum(lhs2, rhs2)
+
+    q_all = jnp.concatenate(
+        [q_left, q_mate, q_far0, q_far1, q_far_mate0, q_far_mate1], axis=0
     )
-    gram = lax.psum_scatter(part, "col", scatter_dimension=0, tiled=True)
-    p1 = gram[:, :rows]
-    p2 = gram[:, rows : 2 * rows]
-    p3 = gram[:, 2 * rows :]
+    q_cols = lax.dynamic_slice_in_dim(q_all, r * rows, rows, 1)
+    act_all = jnp.concatenate([own, mate, far, far_mate], axis=0)
+    precond = (dot_tn(q_cols, act_all) * q_right[None, :]).astype(bf16)
+    p2, precond = lax.optimization_barrier((p2, precond))
+
+    got3 = lax.ppermute(p3, "row", [(2, 0), (3, 1)])
     got2 = lax.ppermute(p2, "row", [(3, 0)])
-    got3 = lax.ppermute(p3, "row", [(2, 0), (3, 1)])
     zero = jnp.zeros_like(p1)
     row_ids = c * piece + lax.broadcasted_iota(jnp.int32, p1.shape, 0)
     col_ids = lax.broadcasted_iota(jnp.int32, p1.shape, 1)
@@ -80,15 +108,10 @@
         ],
         axis=1,
     )
-    q_all = jnp.concatenate([q_left, q_mate, q_far, q_far_mate], axis=0)
     ratio = (dot_nn(upper, q_all) / scale).astype(bf16)
     ratio = lax.all_to_all(ratio, "col", split_axis=1, concat_axis=0, tiled=True)
     q_tile = lax.dynamic_slice_in_dim(q_left, c * width, width, 1).astype(f32)
     new_left = q_tile - step_rate * (ratio.astype(f32) - q_tile)
-
-    q_cols = lax.dynamic_slice_in_dim(q_all, r * rows, rows, 1)
-    act_all = jnp.concatenate([own, mate, far, far_mate], axis=0)
-    precond = (dot_tn(q_cols, act_all) * q_right[None, :]).astype(bf16)
     return (new_left, precond)
 
 

time: 478 us -> 478 us (level)
  blocking collectives: 40 us -> 0 us
  local copies, waits for them, and re-layouts: 44.4 us -> 67.3 us
  starting transfers between devices: 10.9 us -> 23 us
  waiting for transfers between devices: 245 us -> 253 us
  other arithmetic: 14.3 us -> 8.43 us
    all_gather x2, waiting for transfers between devices: 174 us -> 8.62 us  [far_half(): return lax.all_gather(swap(mine, 2), 'col', axis=0, tiled=True)]
    reduce_scatter x0 -> x3, waiting for transfers between devices: none -> 107 us  [col_sum(): lax.psum_scatter(dot_nt(a, b).astype(bf16), 'col', scatter_dimension=0, t...]
    ppermute x5 -> x13, waiting for transfers between devices: 40 us -> 107 us  [swap(): return lax.ppermute(x, 'row', [(i, i ^ by) for i in range(4)])]
    psum x1 -> x0, blocking collectives: 40 us -> none  [shards(): total_sq = lax.psum(jnp.sum(own_f * own_f), ('col', 'row'))]
    unnamed x4 -> x5, waiting for transfers between devices: 25.2 us -> 0.08 us
    all_to_all x1, waiting for transfers between devices: 0.01 us -> 24.8 us  [shards(): lax.all_to_all(ratio, 'col', split_axis=1, concat_axis=0, tiled=True)]
    dynamic_update_slice x0 -> x4, local copies, waits for them, and re-layouts: none -> 16.7 us  [shards(): lax.dynamic_update_slice_in_dim(grad_all, block, (r ^ by) * rows, 0)]
    concatenate x1 -> x0, other arithmetic: 11.2 us -> none  [shards(): jnp.concatenate([dot_nt(own, own).astype(bf16), dot_nt(lhs2, rhs2).astype...]
  transfers between devices with their start and end apart: 11 -> 24, of which waited for: 6 -> 12; matrix products, arithmetic and copies ran while one was open for 25% -> 33% of each run, Pallas kernels for 0% -> 0%
where the time goes in v2:
time: 478 us; the launch traced here: 477 us
  waiting for transfers between devices  253 us (53%)
  matrix products  109 us (23%)
  local copies, waits for them, and re-layouts  67.3 us (14%)
  starting transfers between devices  23 us (5%)
  between operations  17.4 us (4%)
  other arithmetic  8.43 us (2%)
    ppermute x13, waiting for transfers between devices, swap(): return lax.ppermute(x, 'row', [(i, i ^ by) for i in range(4)])  107 us
    reduce_scatter x3, waiting for transfers between devices, col_sum(): lax.psum_scatter(dot_nt(a, b).astype(bf16), 'col', scatter_dimension=0, t...  107 us
    dot_general x4, matrix products, dot_nn(): lax.dot_general(a, b, (((1,), (0,)), ((), ())), preferred_element_type=f32)  67.8 us
    unnamed x27, local copies, waits for them, and re-layouts  33.6 us
    all_to_all x1, waiting for transfers between devices, shards(): lax.all_to_all(ratio, 'col', split_axis=1, concat_axis=0, tiled=True)  24.8 us
    dot_general x1, matrix products, dot_tn(): lax.dot_general(a, b, (((0,), (0,)), ((), ())), preferred_element_type=f32)  23 us
    dot_general x3, matrix products, dot_nt(): lax.dot_general(a, b, (((1,), (1,)), ((), ())), preferred_element_type=f32)  17.7 us
    dynamic_update_slice x4, local copies, waits for them, and re-layouts, shards(): lax.dynamic_update_slice_in_dim(grad_all, block, (r ^ by) * rows, 0)  16.7 us
  transfers between devices with their start and end apart: 24, of which 12 were waited for; matrix products, arithmetic and copies ran while one was open for 33% of the time, Pallas kernels for 0%

profile of v2, /device:TPU:0, one launch (start us, length us, event | category | flops | bytes accessed | tf_op | source)
XLA Modules:
  0.0 477.1 jit_solution(6295720471834574471)
XLA Ops:
  8.5 3.0 collective-permute-start.3
  11.5 11.9 %collective-permute-done.3 = bf16[64,4096]{1,0:T(8,128)(2,1)S(1)} collective-permute-done((bf16[64,4096]{1,0:T(8,128)(2,1)S(1)}, bf16[64,4096]{1,0:T(8,128)(2,1)S(1)}, u32[]{:S(2)}, u32[]{:S(2)}) %collective-permute-start.3) | collective-permute-done | bytes 524320 | tf_op jit(solution)/shard_map/ppermute | solution.py:25
  26.1 79.1 %collective-permute-done.1 = bf16[1024,1792]{1,0:T(8,128)(2,1)} collective-permute-done((bf16[1024,1792]{1,0:T(8,128)(2,1)}, bf16[1024,1792]{1,0:T(8,128)(2,1)}, u32[]{:S(2)}, u32[]{:S(2)}) %collective-permute-start.1) | collective-permute-done | bytes 3670048 | tf_op jit(solution)/shard_map/ppermute | solution.py:25
  106.6 6.2 %broadcast_in_dim.4 = bf16[4096,1792]{1,0:T(8,128)(2,1)} broadcast(bf16[]{:T(256)} %constant.16.clone.1), dimensions={} | broadcast | bytes 14680066 | tf_op jit(solution)/shard_map/broadcast_in_dim | solution.py:47
  112.8 4.1 constant_dynamic-update-slice_fusion.17
  116.8 2.7 collective-permute-done.5
  120.4 4.1 constant_dynamic-update-slice_fusion.16
  124.5 4.2 constant_dynamic-update-slice_fusion.15
  128.7 4.4 constant_dynamic-update-slice_fusion.14
  133.1 22.7 %constant_dynamic-update-slice_fusion.13 = (bf16[4096,1792]{1,0:T(8,128)(2,1)}, bf16[1792,1024]{0,1:T(8,128)(2,1)S(1)}) fusion(f32[1792]{0:T(1024)S(1)} %copy-done.9, bf16[1024,4096]{1,0:T(8,128)(2,1)} %param.3, bf16[4096,1792]{1,0:T(8,128)(2,1)} %constant_dynamic-update-slice_fusion.14), kind=kOutput, calls=%fused_computation.54 | convolution fusion | flops 15036055552 | bytes 30415872 | tf_op jit(solution)/shard_map/dot_general | solution.py:13
  156.3 11.1 %collective-permute-done.7 = bf16[1024,1792]{1,0:T(8,128)(2,1)S(1)} collective-permute-done((bf16[1024,1792]{1,0:T(8,128)(2,1)S(1)}, bf16[1024,1792]{1,0:T(8,128)(2,1)S(1)}, u32[]{:S(2)}, u32[]{:S(2)}) %collective-permute-start.7) | collective-permute-done | bytes 3670048 | tf_op jit(solution)/shard_map/ppermute | solution.py:25
  171.3 15.0 %constant_dynamic-update-slice_fusion.11 = (bf16[4096,1792]{1,0:T(8,128)(2,1)}, bf16[512,1792]{1,0:T(8,128)(2,1)}) fusion(bf16[4096,1792]{1,0:T(8,128)(2,1)} %constant_dynamic-update-slice_fusion.12, f32[1792]{0:T(1024)S(1)} %copy-done.9, bf16[512,4096]{1,0:T(8,128)(2,1)} %all-gather.3.cloned.1.call-done, ...), kind=kOutput, calls=%fused_computation.52 | convolution fusion | flops 7518027776 | bytes 22551552 | tf_op jit(solution)/shard_map/dot_general | solution.py:13
  186.4 8.6 %all-gather.5.cloned.1.call-done = bf16[512,4096]{1,0:T(8,128)(2,1)} async-done(((bf16[64,4096]{1,0:T(8,128)(2,1)}), bf16[512,4096]{1,0:T(8,128)(2,1)}) %all-gather.5.cloned.1.call-update) | async-done | bytes 4194320 | tf_op jit(solution)/shard_map/all_gather | solution.py:40
  195.1 15.0 %constant_dynamic-update-slice_fusion.10 = (bf16[4096,1792]{1,0:T(8,128)(2,1)}, bf16[512,1792]{1,0:T(8,128)(2,1)}) fusion(bf16[4096,1792]{1,0:T(8,128)(2,1)} %get-tuple-element.16, f32[1792]{0:T(1024)S(1)} %copy-done.9, bf16[512,4096]{1,0:T(8,128)(2,1)} %all-gather.5.cloned.1.call-done, bf16[4096,1792]{1,0:T(8,128)(2,1)} %constant_dynamic-update-slice_fusion.14), kind=kOutput, calls=%fused_computation.51 | convolution fusion | flops 7518027776 | bytes 22551552 | tf_op jit(solution)/shard_map/dot_general | solution.py:13
  210.0 7.3 %fusion.22 = bf16[1024,512]{1,0:T(8,128)(2,1)} fusion(bf16[512,1792]{1,0:T(8,128)(2,1)} %get-tuple-element.17, bf16[1024,1792]{1,0:T(8,128)(2,1)} %bitcast.30, pred[]{:T(512)S(6)} %ge.8, bf16[512,1792]{1,0:T(8,128)(2,1)} %get-tuple-element.19), kind=kOutput, calls=%fused_computation.27 | convolution fusion | flops 1889665024 | bytes 12059648 | tf_op jit(solution)/shard_map/dot_general | solution.py:17
  218.9 3.8 constant_dynamic-update-slice_fusion.8
  222.7 5.2 %fusion.16 = bf16[1024,1024]{1,0:T(8,128)(2,1)} fusion(bf16[1024,1792]{1,0:T(8,128)(2,1)S(1)} %copy-done.3, bf16[1024,1792]{1,0:T(8,128)(2,1)S(1)} %get-tuple-element.9, pred[]{:T(512)S(6)} %eq.15, pred[]{:T(512)S(6)} %eq.16, bf16[1792,1024]{0,1:T(8,128)(2,1)S(1)} %copy-done.5), kind=kOutput, calls=%fused_computation.23 | convolution fusion | flops 3764649984 | bytes 13107202 | tf_op jit(solution)/shard_map/dot_general | solution.py:17
  228.7 8.0 %constant_dynamic-update-slice_fusion.7 = bf16[4096,4096]{1,0:T(8,128)(2,1)} fusion(bf16[1024,4096]{1,0:T(8,128)(2,1)} %param.3), kind=kLoop, calls=%fused_computation.48 | loop fusion | bytes 16777216
  236.6 2.5 multiply_reduce_fusion
  239.6 5.2 %convolution_convert_fusion = bf16[1024,1024]{1,0:T(8,128)(2,1)} fusion(bf16[1792,1024]{0,1:T(8,128)(2,1)S(1)} %copy-done.6), kind=kOutput, calls=%fused_computation.24 | convolution fusion | flops 3759144960 | bytes 5767168 | tf_op jit(solution)/shard_map/dot_general | solution.py:17
  258.9 3.0 collective-permute-start.17
  264.1 8.0 %constant_dynamic-update-slice_fusion.6 = bf16[4096,4096]{1,0:T(8,128)(2,1)} fusion(bf16[4096,4096]{1,0:T(8,128)(2,1)} %constant_dynamic-update-slice_fusion.7, bf16[1024,4096]{1,0:T(8,128)(2,1)} %collective-permute-done.8), kind=kLoop, calls=%fused_computation.47 | loop fusion | bytes 16777216
  272.1 2.4 constant_dynamic-update-slice_fusion.5
  278.2 4.7 constant_dynamic-update-slice_fusion.3
  282.9 4.7 constant_dynamic-update-slice_fusion.2
  287.6 23.0 %multiply_convert_fusion = bf16[1024,1792]{1,0:T(8,128)(2,1)} fusion(bf16[4096,1792]{1,0:T(8,128)(2,1)} %get-tuple-element.8, bf16[4096,4096]{1,0:T(8,128)(2,1)} %constant_dynamic-update-slice_fusion.2, s32[]{:T(128)S(6)} %select_n.92, f32[1792]{0:T(1024)S(1)} %copy-done.9), kind=kOutput, calls=%fused_computation.3 | convolution fusion | flops 15036055552 | bytes 26745860 | tf_op jit(solution)/shard_map/dot_general | solution.py:21
  311.8 37.8 %reduce-scatter.6.cloned.1.call-done = bf16[128,1024]{1,0:T(8,128)(2,1)} async-done(((bf16[1024,1024]{1,0:T(8,128)(2,1)}), bf16[128,1024]{1,0:T(8,128)(2,1)}) %reduce-scatter.6.cloned.1.call-update) | async-done | bytes 262160 | tf_op jit(solution)/shard_map/reduce_scatter | solution.py:83
  350.9 69.2 %reduce-scatter.4.cloned.1.call-done = bf16[128,1024]{1,0:T(8,128)(2,1)} async-done(((bf16[1024,1024]{1,0:T(8,128)(2,1)}), bf16[128,1024]{1,0:T(8,128)(2,1)}) %reduce-scatter.4.cloned.1.call-update) | async-done | bytes 262160 | tf_op jit(solution)/shard_map/reduce_scatter | solution.py:83
  423.1 15.1 %fusion.4 = bf16[128,4096]{1,0:T(8,128)(2,1)S(1)} fusion(bf16[4096,4096]{1,0:T(8,128)(2,1)} %constant_dynamic-update-slice_fusion.2, bf16[128,1024]{1,0:T(8,128)(2,1)S(1)} %get-tuple-element.13, bf16[128,1024]{1,0:T(8,128)(2,1)S(1)} %maximum_select_fusion.4, bf16[128,1024]{1,0:T(8,128)(2,1)S(1)} %get-tuple-element.12, bf16[128,1024]{1,0:T(8,128)(2,1)S(1)} %fusion.30, ...), kind=kOutput, calls=%fused_computation.6 | convolution fusion | flops 4300210176 | bytes 35651588 | tf_op jit(solution)/shard_map/dot_general | solution.py:13
  439.3 3.6 all-to-all-start
  442.9 24.8 %all-to-all-done = bf16[128,8,512]{2,0,1:T(8,128)(2,1)S(1)} async-done(((bf16[128,8,512]{2,0,1:T(8,128)(2,1)}), bf16[128,8,512]{2,0,1:T(8,128)(2,1)S(1)}, u32[]{:S(2)}, u32[]{:S(2)}) %all-to-all-start) | async-done | bytes 1048608 | tf_op jit(solution)/shard_map/all_to_all | solution.py:112
  467.7 2.9 convert_subtract_fusion
  (71 shorter events, 36.6 us)
Async XLA Ops:
  7.2 164.1 %all-gather.3.cloned.1.call-start = ((), (), s32[]{:S(2)}) async-start(), calls=%async_computation.5 | async-start | bytes 4718592 | tf_op jit(solution)/shard_map/all_gather | solution.py:40
  8.5 14.9 %collective-permute-start.3 = (bf16[64,4096]{1,0:T(8,128)(2,1)S(1)}, bf16[64,4096]{1,0:T(8,128)(2,1)S(1)}, u32[]{:S(2)}, u32[]{:S(2)}) collective-permute-start(bf16[64,4096]{1,0:T(8,128)(2,1)S(1)} %get-tuple-element.7), channel_id=1, source_target_pairs={{0,2},{1,3},{2,0},{3,1},{4,6},{5,7},{6,4},{7,5},{8,10},{9,11},{10,... | collective-permute-start | bytes 1572872 | tf_op jit(solution)/shard_map/ppermute | solution.py:25
  24.2 170.8 %all-gather.5.cloned.1.call-start = ((), (), s32[]{:S(2)}) async-start(), calls=%async_computation.6 | async-start | bytes 4718592 | tf_op jit(solution)/shard_map/all_gather | solution.py:40
  24.3 80.9 %collective-permute-start.1 = (bf16[1024,1792]{1,0:T(8,128)(2,1)}, bf16[1024,1792]{1,0:T(8,128)(2,1)}, u32[]{:S(2)}, u32[]{:S(2)}) collective-permute-start(bf16[1024,1792]{1,0:T(8,128)(2,1)} %param.4), channel_id=1, source_target_pairs={{0,2},{1,3},{2,0},{3,1},{4,6},{5,7},{6,4},{7,5},{8,10},{9,11},{10,... | collective-permute-start | bytes 11010056 | tf_op jit(solution)/shard_map/ppermute | solution.py:25
  26.1 94.3 %collective-permute-start = (bf16[1024,1792]{1,0:T(8,128)(2,1)}, bf16[1024,1792]{1,0:T(8,128)(2,1)}, u32[]{:S(2)}, u32[]{:S(2)}) collective-permute-start(bf16[1024,1792]{1,0:T(8,128)(2,1)} %param.4), channel_id=1, source_target_pairs={{0,1},{1,0},{2,3},{3,2},{4,5},{5,4},{6,7},{7,6},{8,9},{9,8},{10,11... | collective-permute-start | bytes 11010056 | tf_op jit(solution)/shard_map/ppermute | solution.py:25
  105.2 23.5 %collective-permute-start.2 = (bf16[1024,1792]{1,0:T(8,128)(2,1)}, bf16[1024,1792]{1,0:T(8,128)(2,1)}, u32[]{:S(2)}, u32[]{:S(2)}) collective-permute-start(bf16[1024,1792]{1,0:T(8,128)(2,1)} %collective-permute-done.1), channel_id=1, source_target_pairs={{0,1},{1,0},{2,3},{3,2},{4,5},{5,4},{6,7},{7,6},{8,9},{9,8},{10,11... | collective-permute-start | bytes 11010056 | tf_op jit(solution)/shard_map/ppermute | solution.py:25
  105.2 14.3 %collective-permute-start.5 = (bf16[64,4096]{1,0:T(8,128)(2,1)S(1)}, bf16[64,4096]{1,0:T(8,128)(2,1)S(1)}, u32[]{:S(2)}, u32[]{:S(2)}) collective-permute-start(bf16[64,4096]{1,0:T(8,128)(2,1)S(1)} %get-tuple-element.6), channel_id=1, source_target_pairs={{0,2},{1,3},{2,0},{3,1},{4,6},{5,7},{6,4},{7,5},{8,10},{9,11},{10,... | collective-permute-start | bytes 1572872 | tf_op jit(solution)/shard_map/ppermute | solution.py:25
  120.4 190.2 %reduce-scatter.8.cloned.1.call-start = ((), (), s32[]{:S(2)}) async-start(), calls=%async_computation.8 | async-start | bytes 1179648 | tf_op jit(solution)/shard_map/reduce_scatter | solution.py:83
  128.7 4.4 copy-start.9
  155.8 11.6 %copy-start.4 = (bf16[1792,1024]{0,1:T(8,128)(2,1)}, bf16[1792,1024]{0,1:T(8,128)(2,1)S(1)}, u32[]{:S(2)}) copy-start(bf16[1792,1024]{0,1:T(8,128)(2,1)S(1)} %get-tuple-element.15) | copy-start | bytes 11010052
  155.8 11.6 %collective-permute-start.7 = (bf16[1024,1792]{1,0:T(8,128)(2,1)S(1)}, bf16[1024,1792]{1,0:T(8,128)(2,1)S(1)}, u32[]{:S(2)}, u32[]{:S(2)}) collective-permute-start(bf16[1024,1792]{1,0:T(8,128)(2,1)S(1)} %bitcast.29), channel_id=1, source_target_pairs={{0,1},{1,0},{2,3},{3,2},{4,5},{5,4},{6,7},{7,6},{8,9},{9,8},{10,11... | collective-permute-start | bytes 11010056 | tf_op jit(solution)/shard_map/ppermute | solution.py:25
  155.8 108.3 %collective-permute-start.8 = (bf16[1024,4096]{1,0:T(8,128)(2,1)}, bf16[1024,4096]{1,0:T(8,128)(2,1)}, u32[]{:S(2)}, u32[]{:S(2)}) collective-permute-start(bf16[1024,4096]{1,0:T(8,128)(2,1)} %param.3), channel_id=1, source_target_pairs={{0,1},{1,0},{2,3},{3,2},{4,5},{5,4},{6,7},{7,6},{8,9},{9,8},{10,11... | collective-permute-start | bytes 25165832 | tf_op jit(solution)/shard_map/ppermute | solution.py:25
  167.4 1.8 copy-start.2
  186.3 31.1 %collective-permute-start.4 = (bf16[512,1792]{1,0:T(8,128)(2,1)}, bf16[512,1792]{1,0:T(8,128)(2,1)S(1)}, u32[]{:S(2)}, u32[]{:S(2)}) collective-permute-start(bf16[512,1792]{1,0:T(8,128)(2,1)} %get-tuple-element.17), channel_id=1, source_target_pairs={{0,1},{1,0},{2,3},{3,2},{4,5},{5,4},{6,7},{7,6},{8,9},{9,8},{10,11... | collective-permute-start | bytes 5505032 | tf_op jit(solution)/shard_map/ppermute | solution.py:25
  210.0 8.9 %collective-permute-start.6 = (bf16[512,1792]{1,0:T(8,128)(2,1)}, bf16[512,1792]{1,0:T(8,128)(2,1)}, u32[]{:S(2)}, u32[]{:S(2)}) collective-permute-start(bf16[512,1792]{1,0:T(8,128)(2,1)} %get-tuple-element.19), channel_id=1, source_target_pairs={{0,1},{1,0},{2,3},{3,2},{4,5},{5,4},{6,7},{7,6},{8,9},{9,8},{10,11... | collective-permute-start | bytes 5505032 | tf_op jit(solution)/shard_map/ppermute | solution.py:25
  217.4 132.2 %reduce-scatter.6.cloned.1.call-start = ((), (), s32[]{:S(2)}) async-start(), calls=%async_computation.7 | async-start | bytes 2359296 | tf_op jit(solution)/shard_map/reduce_scatter | solution.py:83
  217.4 5.3 %copy-start.3 = (bf16[1024,1792]{1,0:T(8,128)(2,1)S(1)}, bf16[1024,1792]{1,0:T(8,128)(2,1)}, u32[]{:S(2)}) copy-start(bf16[1024,1792]{1,0:T(8,128)(2,1)} %copy-done.2) | copy-start | bytes 11010052
  217.4 5.3 %copy-start.5 = (bf16[1792,1024]{0,1:T(8,128)(2,1)S(1)}, bf16[1792,1024]{0,1:T(8,128)(2,1)}, u32[]{:S(2)}) copy-start(bf16[1792,1024]{0,1:T(8,128)(2,1)} %copy-done.4) | copy-start | bytes 11010052
  227.9 192.1 %reduce-scatter.4.cloned.1.call-start = ((), (), s32[]{:S(2)}) async-start(), calls=%async_computation.4 | async-start | bytes 2359296 | tf_op jit(solution)/shard_map/reduce_scatter | solution.py:83
  228.0 50.2 %collective-permute-start.9 = (bf16[512,4096]{1,0:T(8,128)(2,1)}, bf16[512,4096]{1,0:T(8,128)(2,1)}, u32[]{:S(2)}, u32[]{:S(2)}) collective-permute-start(bf16[512,4096]{1,0:T(8,128)(2,1)} %all-gather.3.cloned.1.call-done), channel_id=1, source_target_pairs={{0,1},{1,0},{2,3},{3,2},{4,5},{5,4},{6,7},{7,6},{8,9},{9,8},{10,11... | collective-permute-start | bytes 12582920 | tf_op jit(solution)/shard_map/ppermute | solution.py:25
  228.6 8.1 %copy-start.6 = (bf16[1792,1024]{0,1:T(8,128)(2,1)S(1)}, bf16[1792,1024]{0,1:T(8,128)(2,1)}, u32[]{:S(2)}) copy-start(bf16[1792,1024]{0,1:T(8,128)(2,1)} %copy-done.4) | copy-start | bytes 11010052
  228.6 54.3 %collective-permute-start.10 = (bf16[512,4096]{1,0:T(8,128)(2,1)}, bf16[512,4096]{1,0:T(8,128)(2,1)}, u32[]{:S(2)}, u32[]{:S(2)}) collective-permute-start(bf16[512,4096]{1,0:T(8,128)(2,1)} %all-gather.5.cloned.1.call-done), channel_id=1, source_target_pairs={{0,1},{1,0},{2,3},{3,2},{4,5},{5,4},{6,7},{7,6},{8,9},{9,8},{10,11... | collective-permute-start | bytes 12582920 | tf_op jit(solution)/shard_map/ppermute | solution.py:25
  239.1 5.8 %collective-permute-start.13 = (f32[1,1]{1,0:T(1,128)}, f32[1,1]{1,0:T(1,128)}, u32[]{:S(2)}, u32[]{:S(2)}) collective-permute-start(f32[1,1]{1,0:T(1,128)} %bitcast.1), channel_id=1, source_target_pairs={{0,1},{1,0},{2,3},{3,2},{4,5},{5,4},{6,7},{7,6},{8,9},{9,8},{10,11... | collective-permute-start | bytes 20 | tf_op jit(solution)/shard_map/ppermute | solution.py:25
  246.1 3.7 collective-permute-start.14
  250.4 3.7 collective-permute-start.15
  254.7 3.7 collective-permute-start.16
  258.9 4.6 collective-permute-start.17
  264.1 8.0 %copy-start = (bf16[512,4096]{1,0:T(8,128)(2,1)S(1)}, bf16[512,4096]{1,0:T(8,128)(2,1)}, u32[]{:S(2)}) copy-start(bf16[512,4096]{1,0:T(8,128)(2,1)} %all-gather.3.cloned.1.call-done) | copy-start | bytes 12582916
  272.1 3.7 copy-start.1
  310.5 110.6 %collective-permute-start.11 = (bf16[128,512]{1,0:T(8,128)(2,1)}, bf16[128,512]{1,0:T(8,128)(2,1)S(1)}, u32[]{:S(2)}, u32[]{:S(2)}) collective-permute-start(bf16[128,512]{1,0:T(8,128)(2,1)} %reduce-scatter.8.cloned.1.call-done), channel_id=1, source_target_pairs={{2,0},{3,1},{6,4},{7,5},{10,8},{11,9},{14,12},{15,13},{18,16},{19,... | collective-permute-start | bytes 393224 | tf_op jit(solution)/shard_map/ppermute | solution.py:97
  349.6 72.5 %collective-permute-start.12 = (bf16[128,1024]{1,0:T(8,128)(2,1)}, bf16[128,1024]{1,0:T(8,128)(2,1)S(1)}, u32[]{:S(2)}, u32[]{:S(2)}) collective-permute-start(bf16[128,1024]{1,0:T(8,128)(2,1)} %reduce-scatter.6.cloned.1.call-done), channel_id=1, source_target_pairs={{3,0},{7,4},{11,8},{15,12},{19,16},{23,20},{27,24},{31,28}} | collective-permute-start | bytes 786440 | tf_op jit(solution)/shard_map/ppermute | solution.py:98
  439.3 28.4 %all-to-all-start = ((bf16[128,8,512]{2,0,1:T(8,128)(2,1)}), bf16[128,8,512]{2,0,1:T(8,128)(2,1)S(1)}, u32[]{:S(2)}, u32[]{:S(2)}) async-start(bf16[128,8,512]{2,0,1:T(8,128)(2,1)} %bitcast.28), calls=%async_computation.3 | async-start | bytes 2097152 | tf_op jit(solution)/shard_map/all_to_all | solution.py:112
  (2 other events, 1.6 us)
Sparse Core Ops, SparseCore 0:
  24.4 74.8 all-gather.2
  120.5 74.5 all-gather.4
  217.5 60.9 reduce-scatter.7
  282.8 66.7 reduce-scatter.5
  353.4 66.6 reduce-scatter.3

commit v3 on v1

--- a/solution.py
+++ b/solution.py
@@ -1,6 +1,10 @@
+import functools
+
 import jax
 import jax.numpy as jnp
 from jax import lax
+from jax.experimental import pallas as pl
+from jax.experimental.pallas import tpu as pltpu
 from jax.sharding import PartitionSpec as P
 
 step_rate = 0.5
@@ -23,6 +27,155 @@
 
 def swap(x, by):
     return lax.ppermute(x, "row", [(i, i ^ by) for i in range(4)])
+
+
+def gram_kernel(count, own, mate, far, far_mate, out, act, acc, send, recv, load_sem, send_sem, recv_sem):
+    r = lax.axis_index("row")
+    c = lax.axis_index("col")
+    rows = own.shape[0]
+    half = rows // 2
+    piece, width = send.shape[2], send.shape[3]
+    bits = [1 << i for i in range(count.bit_length() - 1)]
+    orders = (bits, bits[1:2] + bits[:1] + bits[2:])
+
+    loads = [pltpu.make_async_copy(src, act.at[i], load_sem.at[i]) for i, src in enumerate((own, mate, far, far_mate))]
+    for load in loads:
+        load.start()
+
+    def bit_of(bit):
+        return (c // bit) % 2
+
+    def partner(bit):
+        return c + bit - 2 * bit * bit_of(bit)
+
+    barrier = pltpu.get_barrier_semaphore()
+    for bit in bits:
+        pl.semaphore_signal(barrier, inc=1, device_id=(partner(bit), r), device_id_type=pl.DeviceIdType.MESH)
+    pl.semaphore_wait(barrier, len(bits))
+    for load in loads:
+        load.wait()
+
+    odd = r % 2
+    last = r // 3
+    lhs2 = 3 * last
+    rhs2 = (1 - odd) + 3 * odd * (1 - last)
+    low = r // 2
+    lhs3 = 2 * low
+    rhs3 = 2 * (1 - low)
+    tile = 256
+
+    def compute(first, stop):
+        for col in range(first, stop, tile):
+            if col < rows:
+                a, b, at = 0, 0, col
+            elif col < 2 * rows:
+                a, b, at = lhs2, rhs2, col - rows
+            else:
+                a, b, at = lhs3, rhs3, low * half + (col - 2 * rows)
+            right = act[b, pl.ds(pl.multiple_of(at, tile), tile), :]
+
+            @pl.loop(0, rows // tile)
+            def _(i):
+                at_row = pl.ds(pl.multiple_of(i * tile, tile), tile)
+                acc[at_row, col : col + tile] = dot_nt(act[a, at_row, :], right)
+
+    def copy(chain, step, j, group):
+        slot = count - (count >> step) + j
+        return pltpu.make_async_remote_copy(
+            src_ref=send.at[chain, group],
+            dst_ref=recv.at[chain, slot],
+            send_sem=send_sem.at[chain, slot],
+            recv_sem=recv_sem.at[chain, slot],
+            device_id=(partner(orders[chain][step]), r),
+            device_id_type=pl.DeviceIdType.MESH,
+        )
+
+    def group_of(chain, step, j, flip):
+        order = orders[chain]
+        group = 0
+        for bit in order[:step]:
+            group = group + bit * bit_of(bit)
+        here = bit_of(order[step])
+        group = group + order[step] * ((1 - here) if flip else here)
+        free = order[step + 1 :]
+        for i, bit in enumerate(reversed(free)):
+            group = group + bit * ((j // (1 << i)) % 2)
+        return group
+
+    def place(chain, group):
+        return (pl.ds(pl.multiple_of(group * piece, piece), piece), slice(chain * width, (chain + 1) * width))
+
+    def take(chain, step, j):
+        group = group_of(chain, step, j, False)
+        copy(chain, step, j, group).wait_recv()
+        at = place(chain, group)
+        acc[at] += recv[chain, count - (count >> step) + j].astype(f32)
+
+    def step_out(chain, step):
+        many = count >> (step + 1)
+
+        @pl.loop(0, many)
+        def _(j):
+            if step:
+                take(chain, step - 1, (1 - bit_of(orders[chain][step])) * many + j)
+            group = group_of(chain, step, j, True)
+            send[chain, group] = acc[place(chain, group)].astype(bf16)
+            copy(chain, step, j, group).start()
+
+    def step_in(chain, step):
+        many = count >> (step + 1)
+
+        @pl.loop(0, many)
+        def _(j):
+            take(chain, step - 1, bit_of(orders[chain][step]) * many + j)
+
+    steps = len(bits)
+    for chain in (0, 1):
+        compute(chain * width, (chain + 1) * width)
+        step_out(chain, 0)
+    for step in range(1, steps):
+        for chain in (0, 1):
+            step_out(chain, step)
+        for chain in (0, 1):
+            step_in(chain, step)
+    for chain in (0, 1):
+        take(chain, steps - 1, 0)
+        at = place(chain, c)
+        out[:, chain * width : (chain + 1) * width] = acc[at].astype(bf16)
+    for chain in (0, 1):
+        for step in range(steps):
+
+            @pl.loop(0, count >> (step + 1))
+            def _(j):
+                copy(chain, step, j, group_of(chain, step, j, True)).wait_send()
+
+
+def gram_sum(own, mate, far, far_mate, count):
+    rows, depth = own.shape
+    total = 5 * rows // 2
+    piece = rows // count
+    width = total // 2
+    return pl.pallas_call(
+        functools.partial(gram_kernel, count),
+        out_shape=jax.ShapeDtypeStruct((piece, total), bf16),
+        in_specs=[pl.BlockSpec(memory_space=pl.ANY)] * 4,
+        out_specs=pl.BlockSpec(memory_space=pltpu.VMEM),
+        scratch_shapes=[
+            pltpu.VMEM((4, rows, depth), bf16),
+            pltpu.VMEM((rows, total), f32),
+            pltpu.VMEM((2, count, piece, width), bf16),
+            pltpu.VMEM((2, count - 1, piece, width), bf16),
+            pltpu.SemaphoreType.DMA((4,)),
+            pltpu.SemaphoreType.DMA((2, count - 1)),
+            pltpu.SemaphoreType.DMA((2, count - 1)),
+        ],
+        compiler_params=pltpu.CompilerParams(
+            collective_id=0, has_side_effects=True, vmem_limit_bytes=56 * 1024 * 1024
+        ),
+        cost_estimate=pl.CostEstimate(
+            flops=2 * rows * total * depth, bytes_accessed=8 * rows * depth, transcendentals=0
+        ),
+    )(own, mate, far, far_mate)
 
 
 def shards(q_left, grad, q_right):
@@ -33,11 +186,15 @@
     assert lax.axis_size("row") == 4
     piece = rows // col_count
     width = order // col_count
-    half = rows // 2
-
-    grad_all = lax.all_gather(grad, "row", axis=0, tiled=True)
+
     q_far_piece = swap(lax.dynamic_slice_in_dim(q_left, c * piece, piece, 0), 2)
     q_far = lax.all_gather(q_far_piece, "col", axis=0, tiled=True)
+    grad_far = swap(grad, 2)
+    grad_mate = swap(grad, 1)
+    grad_far_mate = swap(grad_far, 1)
+    grad_all = jnp.zeros((order,) + grad.shape[1:], grad.dtype)
+    for by, block in ((0, grad), (1, grad_mate), (2, grad_far), (3, grad_far_mate)):
+        grad_all = lax.dynamic_update_slice_in_dim(grad_all, block, (r ^ by) * rows, 0)
     q_mate = swap(q_left, 1)
     q_far_mate = swap(q_far, 1)
 
@@ -45,29 +202,27 @@
         return (dot_nn(q, grad_all) * q_right[None, :]).astype(bf16)
 
     own = act_of(q_left)
+    mate = swap(own, 1)
     far = act_of(q_far)
-    mate = swap(own, 1)
     far_mate = swap(far, 1)
 
     own_f = own.astype(f32)
-    total_sq = lax.psum(jnp.sum(own_f * own_f), ("col", "row"))
+    total_sq = jnp.sum(own_f * own_f).reshape(1, 1)
+    total_sq = total_sq + swap(total_sq, 1)
+    total_sq = total_sq + swap(total_sq, 2)
+    by = 1
+    while by < col_count:
+        total_sq = total_sq + lax.ppermute(total_sq, "col", [(i, i ^ by) for i in range(col_count)])
+        by *= 2
     scale = total_sq / order + epsilon
 
     even = (r % 2) == 0
-    lhs2 = jnp.where(r == 3, far_mate, own)
-    rhs2 = jnp.where(even, mate, jnp.where(r == 3, own, far_mate))
-    lhs3 = jnp.where(r >= 2, far, own)
-    rhs3 = jnp.where(r >= 2, own[half:], far[:half])
-    part = jnp.concatenate(
-        [dot_nt(own, own).astype(bf16), dot_nt(lhs2, rhs2).astype(bf16), dot_nt(lhs3, rhs3).astype(bf16)],
-        axis=1,
-    )
-    gram = lax.psum_scatter(part, "col", scatter_dimension=0, tiled=True)
+    gram = gram_sum(own, mate, far, far_mate, col_count)
     p1 = gram[:, :rows]
     p2 = gram[:, rows : 2 * rows]
     p3 = gram[:, 2 * rows :]
+    got3 = lax.ppermute(p3, "row", [(2, 0), (3, 1)])
     got2 = lax.ppermute(p2, "row", [(3, 0)])
-    got3 = lax.ppermute(p3, "row", [(2, 0), (3, 1)])
     zero = jnp.zeros_like(p1)
     row_ids = c * piece + lax.broadcasted_iota(jnp.int32, p1.shape, 0)
     col_ids = lax.broadcasted_iota(jnp.int32, p1.shape, 1)
@@ -85,7 +240,6 @@
     ratio = lax.all_to_all(ratio, "col", split_axis=1, concat_axis=0, tiled=True)
     q_tile = lax.dynamic_slice_in_dim(q_left, c * width, width, 1).astype(f32)
     new_left = q_tile - step_rate * (ratio.astype(f32) - q_tile)
-
     q_cols = lax.dynamic_slice_in_dim(q_all, r * rows, rows, 1)
     act_all = jnp.concatenate([own, mate, far, far_mate], axis=0)
     precond = (dot_tn(q_cols, act_all) * q_right[None, :]).astype(bf16)

time: 478 us -> 391 us (0.82)
  waiting for transfers between devices: 245 us -> 106 us
  Pallas kernels: 0 us -> 85.9 us
  blocking collectives: 40 us -> 0 us
  matrix products: 108 us -> 87.2 us
  starting transfers between devices: 10.9 us -> 30.4 us
  local copies, waits for them, and re-layouts: 44.4 us -> 59.5 us
  other arithmetic: 14.3 us -> 3.17 us
    all_gather x1, waiting for transfers between devices: 105 us -> 0.01 us  [shards(): q_far = lax.all_gather(q_far_piece, 'col', axis=0, tiled=True)]
    pallas_call x0 -> x1, Pallas kernels: none -> 85.9 us  [gram_sum(): pl.pallas_call(functools.partial(gram_kernel, count), out_shape=jax.Shape...]
    all_gather x1 -> x0, waiting for transfers between devices: 68.1 us -> none  [shards(): grad_all = lax.all_gather(grad, 'row', axis=0, tiled=True)]
    ppermute x5 -> x10, waiting for transfers between devices: 40 us -> 104 us  [swap(): return lax.ppermute(x, 'row', [(i, i ^ by) for i in range(4)])]
    psum x1 -> x0, blocking collectives: 40 us -> none  [shards(): total_sq = lax.psum(jnp.sum(own_f * own_f), ('col', 'row'))]
    unnamed x4 -> x1, waiting for transfers between devices: 25.2 us -> 0.02 us
    dot_general x3 -> x0, matrix products: 20.6 us -> none  [dot_nt(): lax.dot_general(a, b, (((1,), (1,)), ((), ())), preferred_element_type=f32)]
    dynamic_update_slice x0 -> x4, local copies, waits for them, and re-layouts: none -> 17.1 us  [shards(): lax.dynamic_update_slice_in_dim(grad_all, block, (r ^ by) * rows, 0)]
  transfers between devices with their start and end apart: 11 -> 17, of which waited for: 6 -> 7; matrix products, arithmetic and copies ran while one was open for 25% -> 31% of each run, Pallas kernels for 0% -> 22%
where the time goes in v3:
time: 391 us; the launch traced here: 390 us
  waiting for transfers between devices  106 us (27%)
  matrix products  87.2 us (22%)
  Pallas kernels  85.9 us (22%)
  local copies, waits for them, and re-layouts  59.5 us (15%)
  starting transfers between devices  30.4 us (8%)
  between operations  18.2 us (5%)
    ppermute x10, waiting for transfers between devices, swap(): return lax.ppermute(x, 'row', [(i, i ^ by) for i in range(4)])  104 us
    pallas_call x1, Pallas kernels, gram_sum(): pl.pallas_call(functools.partial(gram_kernel, count), out_shape=jax.Shape...  85.9 us
    dot_general x3, matrix products, dot_nn(): lax.dot_general(a, b, (((1,), (0,)), ((), ())), preferred_element_type=f32)  60.7 us
    dot_general x1, matrix products, dot_tn(): lax.dot_general(a, b, (((0,), (0,)), ((), ())), preferred_element_type=f32)  26.5 us
    unnamed x13, local copies, waits for them, and re-layouts  24.2 us
    dynamic_update_slice x4, local copies, waits for them, and re-layouts, shards(): lax.dynamic_update_slice_in_dim(grad_all, block, (r ^ by) * rows, 0)  17.1 us
    ppermute x3, starting transfers between devices, shards(): lax.ppermute(total_sq, 'col', [(i, i ^ by) for i in range(col_count)])  9.58 us
    ppermute x10, starting transfers between devices, swap(): return lax.ppermute(x, 'row', [(i, i ^ by) for i in range(4)])  9.13 us
  transfers between devices with their start and end apart: 17, of which 7 were waited for; matrix products, arithmetic and copies ran while one was open for 31% of the time, Pallas kernels for 22%

profile of v3, /device:TPU:0, one launch (start us, length us, event | category | flops | bytes accessed | tf_op | source)
XLA Modules:
  0.0 390.3 jit_solution(16775299470843921851)
XLA Ops:
  7.2 1.3 constant_dynamic-slice_fusion
  8.5 3.0 collective-permute-start.4
  11.5 23.2 %collective-permute-done.4 = bf16[128,4096]{1,0:T(8,128)(2,1)S(1)} collective-permute-done((bf16[128,4096]{1,0:T(8,128)(2,1)S(1)}, bf16[128,4096]{1,0:T(8,128)(2,1)S(1)}, u32[]{:S(2)}, u32[]{:S(2)}) %collective-permute-start.4) | collective-permute-done | bytes 1048608 | tf_op jit(solution)/shard_map/ppermute | solution.py:29
  34.7 1.0 copy-done.1
  35.7 1.8 collective-permute-start.1
  37.5 79.1 %collective-permute-done.1 = bf16[1024,1792]{1,0:T(8,128)(2,1)} collective-permute-done((bf16[1024,1792]{1,0:T(8,128)(2,1)}, bf16[1024,1792]{1,0:T(8,128)(2,1)}, u32[]{:S(2)}, u32[]{:S(2)}) %collective-permute-start.1) | collective-permute-done | bytes 3670048 | tf_op jit(solution)/shard_map/ppermute | solution.py:29
  117.1 6.2 %broadcast_in_dim.4 = bf16[4096,1792]{1,0:T(8,128)(2,1)} broadcast(bf16[]{:T(256)} %constant.14.clone.1), dimensions={} | broadcast | bytes 14680066 | tf_op jit(solution)/shard_map/broadcast_in_dim | solution.py:195
  123.2 4.1 %constant_dynamic-update-slice_fusion.7 = bf16[4096,1792]{1,0:T(8,128)(2,1)} fusion(bf16[4096,1792]{1,0:T(8,128)(2,1)} %broadcast_in_dim.4, bf16[1024,1792]{1,0:T(8,128)(2,1)} %param.4, s32[]{:T(128)S(6)} %select_n.57), kind=kLoop, calls=%fused_computation.41 | loop fusion | bytes 7340036 | tf_op jit(solution)/shard_map/dynamic_update_slice | solution.py:197
  127.3 4.3 %constant_dynamic-update-slice_fusion.6 = bf16[4096,1792]{1,0:T(8,128)(2,1)} fusion(bf16[4096,1792]{1,0:T(8,128)(2,1)} %constant_dynamic-update-slice_fusion.7, bf16[1024,1792]{1,0:T(8,128)(2,1)} %collective-permute-done, s32[]{:T(128)S(6)} %select_n.58), kind=kLoop, calls=%fused_computation.40 | loop fusion | bytes 7340036 | tf_op jit(solution)/shard_map/dynamic_update_slice | solution.py:197
  131.6 4.4 %constant_dynamic-update-slice_fusion.5 = bf16[4096,1792]{1,0:T(8,128)(2,1)} fusion(bf16[4096,1792]{1,0:T(8,128)(2,1)} %constant_dynamic-update-slice_fusion.6, bf16[1024,1792]{1,0:T(8,128)(2,1)} %collective-permute-done.1, s32[]{:T(128)S(6)} %select_n.59), kind=kLoop, calls=%fused_computation.39 | loop fusion | bytes 7340036 | tf_op jit(solution)/shard_map/dynamic_update_slice | solution.py:197
  135.9 4.4 %constant_dynamic-update-slice_fusion.4 = bf16[4096,1792]{1,0:T(8,128)(2,1)} fusion(bf16[4096,1792]{1,0:T(8,128)(2,1)} %constant_dynamic-update-slice_fusion.5, bf16[1024,1792]{1,0:T(8,128)(2,1)} %collective-permute-done.2, s32[]{:T(128)S(6)} %select_n.60), kind=kLoop, calls=%fused_computation.38 | loop fusion | bytes 7340036 | tf_op jit(solution)/shard_map/dynamic_update_slice | solution.py:197
  140.4 22.9 %multiply_reduce_fusion = (f32[]{:T(128)}, bf16[1024,1792]{1,0:T(8,128)(2,1)}) fusion(f32[1792]{0:T(1024)S(1)} %copy-done.2, bf16[1024,4096]{1,0:T(8,128)(2,1)S(1)} %bitcast.18, bf16[4096,1792]{1,0:T(8,128)(2,1)} %constant_dynamic-update-slice_fusion.4), kind=kOutput, calls=%fused_computation.10 | convolution fusion | flops 15041560576 | bytes 26745860 | tf_op jit(solution)/shard_map/dot_general | solution.py:17
  163.8 22.6 %multiply_convert_fusion.1.far = bf16[1024,1792]{1,0:T(8,128)(2,1)} fusion(bf16[1024,4096]{1,0:T(8,128)(2,1)} %all-gather.2.cloned.1.call-done, bf16[4096,1792]{1,0:T(8,128)(2,1)} %constant_dynamic-update-slice_fusion.4, f32[1792]{0:T(1024)S(1)} %copy-done.2), kind=kOutput, calls=%fused_computation.11 | convolution fusion | flops 15036055552 | bytes 26745856 | tf_op jit(solution)/shard_map/dot_general | solution.py:17
  186.5 7.8 %constant_dynamic-update-slice_fusion.3 = bf16[4096,4096]{1,0:T(8,128)(2,1)} fusion(bf16[1024,4096]{1,0:T(8,128)(2,1)} %param.3), kind=kLoop, calls=%fused_computation.35 | loop fusion | bytes 16777216
  194.7 1.0 collective-permute-done.10
  197.0 2.8 collective-permute-start.11
  201.2 2.7 collective-permute-start.12
  205.5 2.9 collective-permute-start.13
  209.7 4.0 %collective-permute-start.14 = (f32[1,1]{1,0:T(1,128)}, f32[1,1]{1,0:T(1,128)}, u32[]{:S(2)}, u32[]{:S(2)}) collective-permute-start(f32[1,1]{1,0:T(1,128)} %add.60), channel_id=1, source_target_pairs={{0,16},{4,20},{8,24},{12,28},{16,0},{20,4},{24,8},{28,12},{1,17},{... | collective-permute-start | bytes 20 | tf_op jit(solution)/shard_map/ppermute | solution.py:215
  214.8 7.7 %constant_dynamic-update-slice_fusion.2 = bf16[4096,4096]{1,0:T(8,128)(2,1)} fusion(bf16[4096,4096]{1,0:T(8,128)(2,1)} %constant_dynamic-update-slice_fusion.3, bf16[1024,4096]{1,0:T(8,128)(2,1)} %collective-permute-done.8), kind=kLoop, calls=%fused_computation.34 | loop fusion | bytes 16777216
  222.6 85.9 %shard_map.50 = bf16[128,2560]{1,0:T(8,128)(2,1)} custom-call(bf16[1024,1792]{1,0:T(8,128)(2,1)} %get-tuple-element.6.own, bf16[1024,1792]{1,0:T(8,128)(2,1)} %collective-permute-done.3.mate, bf16[1024,1792]{1,0:T(8,128)(2,1)} %multiply_convert_fusion.1.far, bf16[1024,1792]{1,0:T(8,128)(2,1)} %collective-permute-done.5.far_mate), custom_call_target="tpu_custom_call" | custom-call | flops 9395240960 | bytes 14680064 | tf_op jit(solution)/shard_map/pallas_call | solution.py:158
  308.5 1.0 slice.10
  309.4 0.9 slice.11
  310.4 1.4 collective-permute-start.7
  311.8 1.3 collective-permute-start.6
  313.1 7.8 %constant_dynamic-update-slice_fusion.1 = bf16[4096,4096]{1,0:T(8,128)(2,1)} fusion(bf16[4096,4096]{1,0:T(8,128)(2,1)} %constant_dynamic-update-slice_fusion.2, bf16[1024,4096]{1,0:T(8,128)(2,1)} %all-gather.2.cloned.1.call-done), kind=kLoop, calls=%fused_computation.33 | loop fusion | bytes 16777216
  321.2 7.7 %constant_dynamic-update-slice_fusion = bf16[4096,4096]{1,0:T(8,128)(2,1)} fusion(bf16[4096,4096]{1,0:T(8,128)(2,1)} %constant_dynamic-update-slice_fusion.1, bf16[1024,4096]{1,0:T(8,128)(2,1)} %collective-permute-done.9), kind=kLoop, calls=%fused_computation.32 | loop fusion | bytes 16777216 | tf_op jit(solution)/shard_map/concatenate | solution.py:238
  328.9 15.1 %fusion.9 = bf16[128,4096]{1,0:T(8,128)(2,1)S(1)} fusion(bf16[4096,4096]{1,0:T(8,128)(2,1)} %constant_dynamic-update-slice_fusion, bf16[128,1024]{1,0:T(8,128)(2,1)S(1)} %get-tuple-element.4, bf16[128,1024]{1,0:T(8,128)(2,1)S(1)} %maximum_select_fusion, bf16[128,1024]{1,0:T(8,128)(2,1)S(1)} %get-tuple-element.3, ...), kind=kOutput, calls=%fused_computation.14 | convolution fusion | flops 4300210176 | bytes 35651588 | tf_op jit(solution)/shard_map/dot_general | solution.py:17
  344.0 1.1 copy.9
  345.1 8.9 %all-to-all-start = ((bf16[128,8,512]{2,0,1:T(8,128)(2,1)}), bf16[128,8,512]{2,0,1:T(8,128)(2,1)S(1)}, u32[]{:S(2)}, u32[]{:S(2)}) async-start(bf16[128,8,512]{2,0,1:T(8,128)(2,1)} %bitcast.16), calls=%async_computation | async-start | bytes 2097152 | tf_op jit(solution)/shard_map/all_to_all | solution.py:240
  354.0 26.5 %multiply_convert_fusion = bf16[1024,1792]{1,0:T(8,128)(2,1)} fusion(f32[1792]{0:T(1024)S(1)} %copy-done.2, bf16[1024,1792]{1,0:T(8,128)(2,1)} %collective-permute-done.5.far_mate, bf16[1024,1792]{1,0:T(8,128)(2,1)} %multiply_convert_fusion.1.far, bf16[1024,1792]{1,0:T(8,128)(2,1)} %collective-permute-done.3.mate, ...), kind=kOutput, calls=%fused_computation.9 | convolution fusion | flops 15094775808 | bytes 26745860 | tf_op jit(solution)/shard_map/dot_general | solution.py:25
  380.6 2.9 convert_subtract_fusion
  (36 shorter events, 4.7 us)
Async XLA Ops:
  7.2 156.2 %all-gather.2.cloned.1.call-start = ((), (), s32[]{:S(2)}) async-start(), calls=%async_computation.1 | async-start | bytes 9437184 | tf_op jit(solution)/shard_map/all_gather | solution.py:191
  8.5 26.2 %collective-permute-start.4 = (bf16[128,4096]{1,0:T(8,128)(2,1)S(1)}, bf16[128,4096]{1,0:T(8,128)(2,1)S(1)}, u32[]{:S(2)}, u32[]{:S(2)}) collective-permute-start(bf16[128,4096]{1,0:T(8,128)(2,1)S(1)} %constant_dynamic-slice_fusion), channel_id=1, source_target_pairs={{0,2},{1,3},{2,0},{3,1},{4,6},{5,7},{6,4},{7,5},{8,10},{9,11},{10,... | collective-permute-start | bytes 3145736 | tf_op jit(solution)/shard_map/ppermute | solution.py:29
  34.7 1.0 copy-start.1
  35.7 80.9 %collective-permute-start.1 = (bf16[1024,1792]{1,0:T(8,128)(2,1)}, bf16[1024,1792]{1,0:T(8,128)(2,1)}, u32[]{:S(2)}, u32[]{:S(2)}) collective-permute-start(bf16[1024,1792]{1,0:T(8,128)(2,1)} %param.4), channel_id=1, source_target_pairs={{0,2},{1,3},{2,0},{3,1},{4,6},{5,7},{6,4},{7,5},{8,10},{9,11},{10,... | collective-permute-start | bytes 11010056 | tf_op jit(solution)/shard_map/ppermute | solution.py:29
  37.5 89.8 %collective-permute-start = (bf16[1024,1792]{1,0:T(8,128)(2,1)}, bf16[1024,1792]{1,0:T(8,128)(2,1)}, u32[]{:S(2)}, u32[]{:S(2)}) collective-permute-start(bf16[1024,1792]{1,0:T(8,128)(2,1)} %param.4), channel_id=1, source_target_pairs={{0,1},{1,0},{2,3},{3,2},{4,5},{5,4},{6,7},{7,6},{8,9},{9,8},{10,11... | collective-permute-start | bytes 11010056 | tf_op jit(solution)/shard_map/ppermute | solution.py:29
  116.6 19.4 %collective-permute-start.2 = (bf16[1024,1792]{1,0:T(8,128)(2,1)}, bf16[1024,1792]{1,0:T(8,128)(2,1)}, u32[]{:S(2)}, u32[]{:S(2)}) collective-permute-start(bf16[1024,1792]{1,0:T(8,128)(2,1)} %collective-permute-done.1), channel_id=1, source_target_pairs={{0,1},{1,0},{2,3},{3,2},{4,5},{5,4},{6,7},{7,6},{8,9},{9,8},{10,11... | collective-permute-start | bytes 11010056 | tf_op jit(solution)/shard_map/ppermute | solution.py:29
  116.6 98.3 %collective-permute-start.8 = (bf16[1024,4096]{1,0:T(8,128)(2,1)}, bf16[1024,4096]{1,0:T(8,128)(2,1)}, u32[]{:S(2)}, u32[]{:S(2)}) collective-permute-start(bf16[1024,4096]{1,0:T(8,128)(2,1)} %param.3), channel_id=1, source_target_pairs={{0,1},{1,0},{2,3},{3,2},{4,5},{5,4},{6,7},{7,6},{8,9},{9,8},{10,11... | collective-permute-start | bytes 25165832 | tf_op jit(solution)/shard_map/ppermute | solution.py:29
  127.3 13.1 %slice-start = ((s8[8388608]{0:T(1024)(128)(4,1)}), s8[4194304]{0:T(1024)(128)(4,1)S(1)}, s32[]{:S(2)}) async-start(s8[8388608]{0:T(1024)(128)(4,1)} %bitcast.17), calls=%async_computation.2 | async-start | bytes 8388608
  131.6 8.8 %slice-start.1 = ((s8[8388608]{0:T(1024)(128)(4,1)}), s8[4194304]{0:T(1024)(128)(4,1)S(1)}, s32[]{:S(2)}) async-start(s8[8388608]{0:T(1024)(128)(4,1)} %bitcast.17), calls=%async_computation.3 | async-start | bytes 8388608
  131.6 8.8 %copy-start.2 = (f32[1792]{0:T(1024)S(1)}, f32[1792]{0:T(1024)}, u32[]{:S(2)}) copy-start(f32[1792]{0:T(1024)} %param.5) | copy-start | bytes 21508
  163.3 59.3 %collective-permute-start.3 = (bf16[1024,1792]{1,0:T(8,128)(2,1)}, bf16[1024,1792]{1,0:T(8,128)(2,1)}, u32[]{:S(2)}, u32[]{:S(2)}) collective-permute-start(bf16[1024,1792]{1,0:T(8,128)(2,1)} %get-tuple-element.6.own), channel_id=1, source_target_pairs={{0,1},{1,0},{2,3},{3,2},{4,5},{5,4},{6,7},{7,6},{8,9},{9,8},{10,11... | collective-permute-start | bytes 11010056 | tf_op jit(solution)/shard_map/ppermute | solution.py:29
  163.4 157.8 %collective-permute-start.9 = (bf16[1024,4096]{1,0:T(8,128)(2,1)}, bf16[1024,4096]{1,0:T(8,128)(2,1)}, u32[]{:S(2)}, u32[]{:S(2)}) collective-permute-start(bf16[1024,4096]{1,0:T(8,128)(2,1)} %all-gather.2.cloned.1.call-done), channel_id=1, source_target_pairs={{0,1},{1,0},{2,3},{3,2},{4,5},{5,4},{6,7},{7,6},{8,9},{9,8},{10,11... | collective-permute-start | bytes 25165832 | tf_op jit(solution)/shard_map/ppermute | solution.py:29
  186.4 36.1 %collective-permute-start.5 = (bf16[1024,1792]{1,0:T(8,128)(2,1)}, bf16[1024,1792]{1,0:T(8,128)(2,1)}, u32[]{:S(2)}, u32[]{:S(2)}) collective-permute-start(bf16[1024,1792]{1,0:T(8,128)(2,1)} %multiply_convert_fusion.1.far), channel_id=1, source_target_pairs={{0,1},{1,0},{2,3},{3,2},{4,5},{5,4},{6,7},{7,6},{8,9},{9,8},{10,11... | collective-permute-start | bytes 11010056 | tf_op jit(solution)/shard_map/ppermute | solution.py:29
  194.3 1.4 collective-permute-start.10
  197.0 3.6 collective-permute-start.11
  201.2 3.6 collective-permute-start.12
  205.5 3.6 collective-permute-start.13
  209.7 4.5 %collective-permute-start.14 = (f32[1,1]{1,0:T(1,128)}, f32[1,1]{1,0:T(1,128)}, u32[]{:S(2)}, u32[]{:S(2)}) collective-permute-start(f32[1,1]{1,0:T(1,128)} %add.60), channel_id=1, source_target_pairs={{0,16},{4,20},{8,24},{12,28},{16,0},{20,4},{24,8},{28,12},{1,17},{... | collective-permute-start | bytes 20 | tf_op jit(solution)/shard_map/ppermute | solution.py:215
  310.3 10.6 %copy-start = (bf16[128,2560]{1,0:T(8,128)(2,1)S(1)}, bf16[128,2560]{1,0:T(8,128)(2,1)}, u32[]{:S(2)}) copy-start(bf16[128,2560]{1,0:T(8,128)(2,1)} %shard_map.50) | copy-start | bytes 1966084
  310.4 10.6 %collective-permute-start.7 = (bf16[128,1024]{1,0:T(8,128)(2,1)S(1)}, bf16[128,1024]{1,0:T(8,128)(2,1)S(1)}, u32[]{:S(2)}, u32[]{:S(2)}) collective-permute-start(bf16[128,1024]{1,0:T(8,128)(2,1)S(1)} %slice.10), channel_id=1, source_target_pairs={{3,0},{7,4},{11,8},{15,12},{19,16},{23,20},{27,24},{31,28}} | collective-permute-start | bytes 786440 | tf_op jit(solution)/shard_map/ppermute | solution.py:225
  311.8 9.1 %collective-permute-start.6 = (bf16[128,512]{1,0:T(8,128)(2,1)S(1)}, bf16[128,512]{1,0:T(8,128)(2,1)S(1)}, u32[]{:S(2)}, u32[]{:S(2)}) collective-permute-start(bf16[128,512]{1,0:T(8,128)(2,1)S(1)} %slice.11), channel_id=1, source_target_pairs={{2,0},{3,1},{6,4},{7,5},{10,8},{11,9},{14,12},{15,13},{18,16},{19,... | collective-permute-start | bytes 393224 | tf_op jit(solution)/shard_map/ppermute | solution.py:224
  345.1 35.5 %all-to-all-start = ((bf16[128,8,512]{2,0,1:T(8,128)(2,1)}), bf16[128,8,512]{2,0,1:T(8,128)(2,1)S(1)}, u32[]{:S(2)}, u32[]{:S(2)}) async-start(bf16[128,8,512]{2,0,1:T(8,128)(2,1)} %bitcast.16), calls=%async_computation | async-start | bytes 2097152 | tf_op jit(solution)/shard_map/all_to_all | solution.py:240
Sparse Core Ops, SparseCore 0:
  35.8 126.4 all-gather.1

commit v4 on v3

--- a/solution.py
+++ b/solution.py
@@ -29,7 +29,7 @@
     return lax.ppermute(x, "row", [(i, i ^ by) for i in range(4)])
 
 
-def gram_kernel(count, own, mate, far, far_mate, out, act, acc, send, recv, load_sem, send_sem, recv_sem):
+def gram_kernel(count, own, mate, far, far_mate, out, act_out, act, acc, send, recv, load_sem, store_sem, send_sem, recv_sem):
     r = lax.axis_index("row")
     c = lax.axis_index("col")
     rows = own.shape[0]
@@ -54,6 +54,9 @@
     pl.semaphore_wait(barrier, len(bits))
     for load in loads:
         load.wait()
+    stores = [pltpu.make_async_copy(act.at[i], act_out.at[i], store_sem.at[i]) for i in range(4)]
+    for store in stores:
+        store.start()
 
     odd = r % 2
     last = r // 3
@@ -149,6 +152,9 @@
             def _(j):
                 copy(chain, step, j, group_of(chain, step, j, True)).wait_send()
 
+    for store in stores:
+        store.wait()
+
 
 def gram_sum(own, mate, far, far_mate, count):
     rows, depth = own.shape
@@ -157,14 +163,18 @@
     width = total // 2
     return pl.pallas_call(
         functools.partial(gram_kernel, count),
-        out_shape=jax.ShapeDtypeStruct((piece, total), bf16),
+        out_shape=(
+            jax.ShapeDtypeStruct((piece, total), bf16),
+            jax.ShapeDtypeStruct((4, rows, depth), bf16),
+        ),
         in_specs=[pl.BlockSpec(memory_space=pl.ANY)] * 4,
-        out_specs=pl.BlockSpec(memory_space=pltpu.VMEM),
+        out_specs=(pl.BlockSpec(memory_space=pltpu.VMEM), pl.BlockSpec(memory_space=pl.ANY)),
         scratch_shapes=[
             pltpu.VMEM((4, rows, depth), bf16),
             pltpu.VMEM((rows, total), f32),
             pltpu.VMEM((2, count, piece, width), bf16),
             pltpu.VMEM((2, count - 1, piece, width), bf16),
+            pltpu.SemaphoreType.DMA((4,)),
             pltpu.SemaphoreType.DMA((4,)),
             pltpu.SemaphoreType.DMA((2, count - 1)),
             pltpu.SemaphoreType.DMA((2, count - 1)),
@@ -217,7 +227,7 @@
     scale = total_sq / order + epsilon
 
     even = (r % 2) == 0
-    gram = gram_sum(own, mate, far, far_mate, col_count)
+    gram, act_all = gram_sum(own, mate, far, far_mate, col_count)
     p1 = gram[:, :rows]
     p2 = gram[:, rows : 2 * rows]
     p3 = gram[:, 2 * rows :]
@@ -226,22 +236,20 @@
     zero = jnp.zeros_like(p1)
     row_ids = c * piece + lax.broadcasted_iota(jnp.int32, p1.shape, 0)
     col_ids = lax.broadcasted_iota(jnp.int32, p1.shape, 1)
-    upper = jnp.concatenate(
-        [
-            jnp.where(col_ids >= row_ids, p1, zero),
-            jnp.where(even, p2, zero),
-            jnp.where(r < 2, jnp.concatenate([p3, got3], axis=1), zero),
-            jnp.where(r == 0, got2, jnp.where(r == 1, p2, zero)),
-        ],
-        axis=1,
-    )
-    q_all = jnp.concatenate([q_left, q_mate, q_far, q_far_mate], axis=0)
-    ratio = (dot_nn(upper, q_all) / scale).astype(bf16)
+    upper = [
+        jnp.where(col_ids >= row_ids, p1, zero),
+        jnp.where(even, p2, zero),
+        jnp.where(r < 2, jnp.concatenate([p3, got3], axis=1), zero),
+        jnp.where(r == 0, got2, jnp.where(r == 1, p2, zero)),
+    ]
+    q_rows = (q_left, q_mate, q_far, q_far_mate)
+    stepped = sum(dot_nn(u, q) for u, q in zip(upper, q_rows))
+    ratio = (stepped / scale).astype(bf16)
     ratio = lax.all_to_all(ratio, "col", split_axis=1, concat_axis=0, tiled=True)
     q_tile = lax.dynamic_slice_in_dim(q_left, c * width, width, 1).astype(f32)
     new_left = q_tile - step_rate * (ratio.astype(f32) - q_tile)
-    q_cols = lax.dynamic_slice_in_dim(q_all, r * rows, rows, 1)
-    act_all = jnp.concatenate([own, mate, far, far_mate], axis=0)
+    q_cols = jnp.concatenate([lax.dynamic_slice_in_dim(q, r * rows, rows, 1) for q in q_rows], axis=0)
+    act_all = act_all.reshape(order, grad.shape[1])
     precond = (dot_tn(q_cols, act_all) * q_right[None, :]).astype(bf16)
     return (new_left, precond)
 

time: 391 us -> 368 us (0.941)
  local copies, waits for them, and re-layouts: 59.5 us -> 38.3 us
  matrix products: 87.2 us -> 80.9 us
    unnamed x13 -> x18, local copies, waits for them, and re-layouts: 24.2 us -> 1.01 us
    dynamic_slice x0 -> x4, local copies, waits for them, and re-layouts: none -> 9.68 us  [shards(): lax.dynamic_slice_in_dim(q, r * rows, rows, 1)]
    concatenate x1 -> x0, local copies, waits for them, and re-layouts: 7.73 us -> none  [shards(): q_all = jnp.concatenate([q_left, q_mate, q_far, q_far_mate], axis=0)]
    dot_general x1, matrix products: 26.5 us -> 22.6 us  [dot_tn(): lax.dot_general(a, b, (((0,), (0,)), ((), ())), preferred_element_type=f32)]
    dot_general x3 -> x6, matrix products: 60.7 us -> 58.2 us  [dot_nn(): lax.dot_general(a, b, (((1,), (0,)), ((), ())), preferred_element_type=f32)]
  transfers between devices with their start and end apart: 17 -> 17, of which waited for: 7 -> 7; matrix products, arithmetic and copies ran while one was open for 31% -> 31% of each run, Pallas kernels for 22% -> 23%
where the time goes in v4:
time: 368 us; the launch traced here: 366 us
  waiting for transfers between devices  109 us (30%)
  Pallas kernels  85.8 us (23%)
  matrix products  80.9 us (22%)
  local copies, waits for them, and re-layouts  38.3 us (10%)
  starting transfers between devices  30.8 us (8%)
  between operations  18 us (5%)
    ppermute x10, waiting for transfers between devices, swap(): return lax.ppermute(x, 'row', [(i, i ^ by) for i in range(4)])  107 us
    pallas_call x1, Pallas kernels, gram_sum(): pl.pallas_call(functools.partial(gram_kernel, count), out_shape=(jax.Shap...  85.8 us
    dot_general x6, matrix products, dot_nn(): lax.dot_general(a, b, (((1,), (0,)), ((), ())), preferred_element_type=f32)  58.2 us
    dot_general x1, matrix products, dot_tn(): lax.dot_general(a, b, (((0,), (0,)), ((), ())), preferred_element_type=f32)  22.6 us
    dynamic_update_slice x4, local copies, waits for them, and re-layouts, shards(): lax.dynamic_update_slice_in_dim(grad_all, block, (r ^ by) * rows, 0)  17 us
    dynamic_slice x4, local copies, waits for them, and re-layouts, shards(): lax.dynamic_slice_in_dim(q, r * rows, rows, 1)  9.68 us
    ppermute x3, starting transfers between devices, shards(): lax.ppermute(total_sq, 'col', [(i, i ^ by) for i in range(col_count)])  9.58 us
    ppermute x10, starting transfers between devices, swap(): return lax.ppermute(x, 'row', [(i, i ^ by) for i in range(4)])  9.19 us
  transfers between devices with their start and end apart: 17, of which 7 were waited for; matrix products, arithmetic and copies ran while one was open for 31% of the time, Pallas kernels for 23%

profile of v4, /device:TPU:0, one launch (start us, length us, event | category | flops | bytes accessed | tf_op | source)
XLA Modules:
  0.0 366.1 jit_solution(12147596642547305937)
XLA Ops:
  7.2 1.3 constant_dynamic-slice_fusion.4
  8.5 3.0 collective-permute-start.4
  11.5 23.2 %collective-permute-done.4 = bf16[128,4096]{1,0:T(8,128)(2,1)S(1)} collective-permute-done((bf16[128,4096]{1,0:T(8,128)(2,1)S(1)}, bf16[128,4096]{1,0:T(8,128)(2,1)S(1)}, u32[]{:S(2)}, u32[]{:S(2)}) %collective-permute-start.4) | collective-permute-done | bytes 1048608 | tf_op jit(solution)/shard_map/ppermute | solution.py:29
  35.7 1.8 collective-permute-start.1
  37.5 79.1 %collective-permute-done.1 = bf16[1024,1792]{1,0:T(8,128)(2,1)} collective-permute-done((bf16[1024,1792]{1,0:T(8,128)(2,1)}, bf16[1024,1792]{1,0:T(8,128)(2,1)}, u32[]{:S(2)}, u32[]{:S(2)}) %collective-permute-start.1) | collective-permute-done | bytes 3670048 | tf_op jit(solution)/shard_map/ppermute | solution.py:29
  117.1 6.1 %broadcast_in_dim.4 = bf16[4096,1792]{1,0:T(8,128)(2,1)} broadcast(bf16[]{:T(256)} %constant.14.clone.1), dimensions={} | broadcast | bytes 14680066 | tf_op jit(solution)/shard_map/broadcast_in_dim | solution.py:205
  123.2 4.0 %constant_dynamic-update-slice_fusion.3 = bf16[4096,1792]{1,0:T(8,128)(2,1)} fusion(bf16[4096,1792]{1,0:T(8,128)(2,1)} %broadcast_in_dim.4, bf16[1024,1792]{1,0:T(8,128)(2,1)} %param.4, s32[]{:T(128)S(6)} %select_n.60), kind=kLoop, calls=%fused_computation.50 | loop fusion | bytes 7340036 | tf_op jit(solution)/shard_map/dynamic_update_slice | solution.py:207
  127.3 4.2 %constant_dynamic-update-slice_fusion.2 = bf16[4096,1792]{1,0:T(8,128)(2,1)} fusion(bf16[4096,1792]{1,0:T(8,128)(2,1)} %constant_dynamic-update-slice_fusion.3, bf16[1024,1792]{1,0:T(8,128)(2,1)} %collective-permute-done, s32[]{:T(128)S(6)} %select_n.61), kind=kLoop, calls=%fused_computation.49 | loop fusion | bytes 7340036 | tf_op jit(solution)/shard_map/dynamic_update_slice | solution.py:207
  131.5 4.4 %constant_dynamic-update-slice_fusion.1 = bf16[4096,1792]{1,0:T(8,128)(2,1)} fusion(bf16[4096,1792]{1,0:T(8,128)(2,1)} %constant_dynamic-update-slice_fusion.2, bf16[1024,1792]{1,0:T(8,128)(2,1)} %collective-permute-done.1, s32[]{:T(128)S(6)} %select_n.62), kind=kLoop, calls=%fused_computation.48 | loop fusion | bytes 7340036 | tf_op jit(solution)/shard_map/dynamic_update_slice | solution.py:207
  135.9 4.4 %constant_dynamic-update-slice_fusion = bf16[4096,1792]{1,0:T(8,128)(2,1)} fusion(bf16[4096,1792]{1,0:T(8,128)(2,1)} %constant_dynamic-update-slice_fusion.1, bf16[1024,1792]{1,0:T(8,128)(2,1)} %collective-permute-done.2, s32[]{:T(128)S(6)} %select_n.63), kind=kLoop, calls=%fused_computation.47 | loop fusion | bytes 7340036 | tf_op jit(solution)/shard_map/dynamic_update_slice | solution.py:207
  140.3 22.9 %multiply_reduce_fusion = (f32[]{:T(128)}, bf16[1024,1792]{1,0:T(8,128)(2,1)}) fusion(f32[1792]{0:T(1024)S(1)} %copy-done.2, bf16[1024,4096]{1,0:T(8,128)(2,1)S(1)} %bitcast.23, bf16[4096,1792]{1,0:T(8,128)(2,1)} %constant_dynamic-update-slice_fusion), kind=kOutput, calls=%fused_computation.9 | convolution fusion | flops 15041560576 | bytes 26745860 | tf_op jit(solution)/shard_map/dot_general | solution.py:17
  163.7 22.6 %multiply_convert_fusion.1.far = bf16[1024,1792]{1,0:T(8,128)(2,1)} fusion(bf16[1024,4096]{1,0:T(8,128)(2,1)} %all-gather.2.cloned.1.call-done, bf16[4096,1792]{1,0:T(8,128)(2,1)} %constant_dynamic-update-slice_fusion, f32[1792]{0:T(1024)S(1)} %copy-done.2), kind=kOutput, calls=%fused_computation.10 | convolution fusion | flops 15036055552 | bytes 26745856 | tf_op jit(solution)/shard_map/dot_general | solution.py:17
  186.4 1.8 constant_dynamic-slice_fusion.3
  188.7 4.4 %collective-permute-done.10 = f32[1,1]{1,0:T(1,128)} collective-permute-done((f32[1,1]{1,0:T(1,128)}, f32[1,1]{1,0:T(1,128)}, u32[]{:S(2)}, u32[]{:S(2)}) %collective-permute-start.10) | collective-permute-done | bytes 36 | tf_op jit(solution)/shard_map/ppermute | solution.py:29
  194.3 2.8 collective-permute-start.11
  198.5 2.7 collective-permute-start.12
  202.7 2.9 collective-permute-start.13
  206.9 4.0 %collective-permute-start.14 = (f32[1,1]{1,0:T(1,128)}, f32[1,1]{1,0:T(1,128)}, u32[]{:S(2)}, u32[]{:S(2)}) collective-permute-start(f32[1,1]{1,0:T(1,128)} %add.75), channel_id=1, source_target_pairs={{0,16},{4,20},{8,24},{12,28},{16,0},{20,4},{24,8},{28,12},{1,17},{... | collective-permute-start | bytes 20 | tf_op jit(solution)/shard_map/ppermute | solution.py:225
  211.9 3.1 constant_dynamic-slice_fusion.2
  215.0 3.1 constant_dynamic-slice_fusion.1
  218.1 85.8 %shard_map.50 = (bf16[128,2560]{1,0:T(8,128)(2,1)}, bf16[4,1024,1792]{2,1,0:T(8,128)(2,1)}) custom-call(bf16[1024,1792]{1,0:T(8,128)(2,1)} %get-tuple-element.7.own, bf16[1024,1792]{1,0:T(8,128)(2,1)} %collective-permute-done.3.mate, bf16[1024,1792]{1,0:T(8,128)(2,1)} %multiply_convert_fusion.1.far, bf16[1024,1792]{1,0:T(8,128)(2,1)} %collective-permute-done.5.far_mate), custom_call_target="tpu_custom_call" | custom-call | flops 9395240960 | bytes 14680064 | tf_op jit(solution)/shard_map/pallas_call | solution.py:164
  306.0 1.6 collective-permute-start.8
  307.6 1.6 collective-permute-start.7
  309.2 4.9 %fusion.22 = f32[128,4096]{1,0:T(8,128)S(1)} fusion(bf16[1024,4096]{1,0:T(8,128)(2,1)} %collective-permute-done.6, pred[]{:T(512)S(6)} %eq.11, bf16[128,2560]{1,0:T(8,128)(2,1)} %get-tuple-element.4), kind=kOutput, calls=%fused_computation.30 | convolution fusion | flops 1073872896 | bytes 10747905 | tf_op jit(solution)/shard_map/dot_general | solution.py:17
  314.1 1.6 convolution_add_fusion.1
  315.8 4.7 %fusion.19 = f32[128,4096]{1,0:T(8,128)S(1)} fusion(bf16[1024,4096]{1,0:T(8,128)(2,1)} %collective-permute-done.9, bf16[128,1024]{1,0:T(8,128)(2,1)S(1)} %collective-permute-done.8, pred[]{:T(512)S(6)} %eq.13, pred[]{:T(512)S(6)} %eq.12, bf16[128,2560]{1,0:T(8,128)(2,1)S(1)} %copy-done), kind=kOutput, calls=%fused_computation.27 | convolution fusion | flops 1074003968 | bytes 11010050 | tf_op jit(solution)/shard_map/dot_general | solution.py:17
  320.5 1.6 fusion.10
  322.1 1.1 copy.12
  323.1 8.8 %all-to-all-start = ((bf16[128,8,512]{2,0,1:T(8,128)(2,1)}), bf16[128,8,512]{2,0,1:T(8,128)(2,1)S(1)}, u32[]{:S(2)}, u32[]{:S(2)}) async-start(bf16[128,8,512]{2,0,1:T(8,128)(2,1)} %bitcast.21), calls=%async_computation | async-start | bytes 2097152 | tf_op jit(solution)/shard_map/all_to_all | solution.py:248
  331.9 1.8 constant_dynamic-slice_fusion
  333.7 22.6 %multiply_convert_fusion = bf16[1024,1792]{1,0:T(8,128)(2,1)} fusion(bf16[4096,1792]{1,0:T(8,128)(2,1)} %bitcast.29, bf16[1024,1024]{1,0:T(8,128)(2,1)S(1)} %constant_dynamic-slice_fusion, bf16[1024,1024]{1,0:T(8,128)(2,1)} %constant_dynamic-slice_fusion.1, bf16[1024,1024]{1,0:T(8,128)(2,1)} %constant_dynamic-slice_fusion.2, ...), kind=kOutput, calls=%fused_computation.8 | convolution fusion | flops 15069609984 | bytes 26745856 | tf_op jit(solution)/shard_map/dot_general | solution.py:25
  356.3 2.9 convert_subtract_fusion
  (47 shorter events, 7.5 us)
Async XLA Ops:
  7.2 156.1 %all-gather.2.cloned.1.call-start = ((), (), s32[]{:S(2)}) async-start(), calls=%async_computation.1 | async-start | bytes 9437184 | tf_op jit(solution)/shard_map/all_gather | solution.py:201
  8.5 26.2 %collective-permute-start.4 = (bf16[128,4096]{1,0:T(8,128)(2,1)S(1)}, bf16[128,4096]{1,0:T(8,128)(2,1)S(1)}, u32[]{:S(2)}, u32[]{:S(2)}) collective-permute-start(bf16[128,4096]{1,0:T(8,128)(2,1)S(1)} %constant_dynamic-slice_fusion.4), channel_id=1, source_target_pairs={{0,2},{1,3},{2,0},{3,1},{4,6},{5,7},{6,4},{7,5},{8,10},{9,11},{10,... | collective-permute-start | bytes 3145736 | tf_op jit(solution)/shard_map/ppermute | solution.py:29
  34.7 1.0 copy-start.1
  35.7 80.9 %collective-permute-start.1 = (bf16[1024,1792]{1,0:T(8,128)(2,1)}, bf16[1024,1792]{1,0:T(8,128)(2,1)}, u32[]{:S(2)}, u32[]{:S(2)}) collective-permute-start(bf16[1024,1792]{1,0:T(8,128)(2,1)} %param.4), channel_id=1, source_target_pairs={{0,2},{1,3},{2,0},{3,1},{4,6},{5,7},{6,4},{7,5},{8,10},{9,11},{10,... | collective-permute-start | bytes 11010056 | tf_op jit(solution)/shard_map/ppermute | solution.py:29
  37.5 89.8 %collective-permute-start = (bf16[1024,1792]{1,0:T(8,128)(2,1)}, bf16[1024,1792]{1,0:T(8,128)(2,1)}, u32[]{:S(2)}, u32[]{:S(2)}) collective-permute-start(bf16[1024,1792]{1,0:T(8,128)(2,1)} %param.4), channel_id=1, source_target_pairs={{0,1},{1,0},{2,3},{3,2},{4,5},{5,4},{6,7},{7,6},{8,9},{9,8},{10,11... | collective-permute-start | bytes 11010056 | tf_op jit(solution)/shard_map/ppermute | solution.py:29
  116.6 19.3 %collective-permute-start.2 = (bf16[1024,1792]{1,0:T(8,128)(2,1)}, bf16[1024,1792]{1,0:T(8,128)(2,1)}, u32[]{:S(2)}, u32[]{:S(2)}) collective-permute-start(bf16[1024,1792]{1,0:T(8,128)(2,1)} %collective-permute-done.1), channel_id=1, source_target_pairs={{0,1},{1,0},{2,3},{3,2},{4,5},{5,4},{6,7},{7,6},{8,9},{9,8},{10,11... | collective-permute-start | bytes 11010056 | tf_op jit(solution)/shard_map/ppermute | solution.py:29
  116.6 95.4 %collective-permute-start.6 = (bf16[1024,4096]{1,0:T(8,128)(2,1)}, bf16[1024,4096]{1,0:T(8,128)(2,1)}, u32[]{:S(2)}, u32[]{:S(2)}) collective-permute-start(bf16[1024,4096]{1,0:T(8,128)(2,1)} %param.3), channel_id=1, source_target_pairs={{0,1},{1,0},{2,3},{3,2},{4,5},{5,4},{6,7},{7,6},{8,9},{9,8},{10,11... | collective-permute-start | bytes 25165832 | tf_op jit(solution)/shard_map/ppermute | solution.py:29
  127.3 13.0 %slice-start = ((s8[8388608]{0:T(1024)(128)(4,1)}), s8[4194304]{0:T(1024)(128)(4,1)S(1)}, s32[]{:S(2)}) async-start(s8[8388608]{0:T(1024)(128)(4,1)} %bitcast.22), calls=%async_computation.2 | async-start | bytes 8388608
  131.5 8.8 %slice-start.1 = ((s8[8388608]{0:T(1024)(128)(4,1)}), s8[4194304]{0:T(1024)(128)(4,1)S(1)}, s32[]{:S(2)}) async-start(s8[8388608]{0:T(1024)(128)(4,1)} %bitcast.22), calls=%async_computation.3 | async-start | bytes 8388608
  131.5 8.8 %copy-start.2 = (f32[1792]{0:T(1024)S(1)}, f32[1792]{0:T(1024)}, u32[]{:S(2)}) copy-start(f32[1792]{0:T(1024)} %param.5) | copy-start | bytes 21508
  163.2 54.9 %collective-permute-start.3 = (bf16[1024,1792]{1,0:T(8,128)(2,1)}, bf16[1024,1792]{1,0:T(8,128)(2,1)}, u32[]{:S(2)}, u32[]{:S(2)}) collective-permute-start(bf16[1024,1792]{1,0:T(8,128)(2,1)} %get-tuple-element.7.own), channel_id=1, source_target_pairs={{0,1},{1,0},{2,3},{3,2},{4,5},{5,4},{6,7},{7,6},{8,9},{9,8},{10,11... | collective-permute-start | bytes 11010056 | tf_op jit(solution)/shard_map/ppermute | solution.py:29
  163.3 152.5 %collective-permute-start.9 = (bf16[1024,4096]{1,0:T(8,128)(2,1)}, bf16[1024,4096]{1,0:T(8,128)(2,1)}, u32[]{:S(2)}, u32[]{:S(2)}) collective-permute-start(bf16[1024,4096]{1,0:T(8,128)(2,1)} %all-gather.2.cloned.1.call-done), channel_id=1, source_target_pairs={{0,1},{1,0},{2,3},{3,2},{4,5},{5,4},{6,7},{7,6},{8,9},{9,8},{10,11... | collective-permute-start | bytes 25165832 | tf_op jit(solution)/shard_map/ppermute | solution.py:29
  186.3 31.8 %collective-permute-start.5 = (bf16[1024,1792]{1,0:T(8,128)(2,1)}, bf16[1024,1792]{1,0:T(8,128)(2,1)}, u32[]{:S(2)}, u32[]{:S(2)}) collective-permute-start(bf16[1024,1792]{1,0:T(8,128)(2,1)} %multiply_convert_fusion.1.far), channel_id=1, source_target_pairs={{0,1},{1,0},{2,3},{3,2},{4,5},{5,4},{6,7},{7,6},{8,9},{9,8},{10,11... | collective-permute-start | bytes 11010056 | tf_op jit(solution)/shard_map/ppermute | solution.py:29
  188.2 4.9 %collective-permute-start.10 = (f32[1,1]{1,0:T(1,128)}, f32[1,1]{1,0:T(1,128)}, u32[]{:S(2)}, u32[]{:S(2)}) collective-permute-start(f32[1,1]{1,0:T(1,128)} %bitcast.1), channel_id=1, source_target_pairs={{0,1},{1,0},{2,3},{3,2},{4,5},{5,4},{6,7},{7,6},{8,9},{9,8},{10,11... | collective-permute-start | bytes 20 | tf_op jit(solution)/shard_map/ppermute | solution.py:29
  194.3 3.6 collective-permute-start.11
  198.5 3.6 collective-permute-start.12
  202.7 3.6 collective-permute-start.13
  206.9 4.5 %collective-permute-start.14 = (f32[1,1]{1,0:T(1,128)}, f32[1,1]{1,0:T(1,128)}, u32[]{:S(2)}, u32[]{:S(2)}) collective-permute-start(f32[1,1]{1,0:T(1,128)} %add.75), channel_id=1, source_target_pairs={{0,16},{4,20},{8,24},{12,28},{16,0},{20,4},{24,8},{28,12},{1,17},{... | collective-permute-start | bytes 20 | tf_op jit(solution)/shard_map/ppermute | solution.py:225
  304.9 9.2 %slice-start.2 = ((s8[8388608]{0:T(1024)(128)(4,1)}), s8[4194304]{0:T(1024)(128)(4,1)S(1)}, s32[]{:S(2)}) async-start(s8[8388608]{0:T(1024)(128)(4,1)} %bitcast.24), calls=%async_computation.4 | async-start | bytes 8388608
  306.0 8.1 %slice-start.3 = ((s8[8388608]{0:T(1024)(128)(4,1)}), s8[4194304]{0:T(1024)(128)(4,1)S(1)}, s32[]{:S(2)}) async-start(s8[8388608]{0:T(1024)(128)(4,1)} %bitcast.24), calls=%async_computation.5 | async-start | bytes 8388608
  306.0 8.1 %copy-start = (bf16[128,2560]{1,0:T(8,128)(2,1)S(1)}, bf16[128,2560]{1,0:T(8,128)(2,1)}, u32[]{:S(2)}) copy-start(bf16[128,2560]{1,0:T(8,128)(2,1)} %get-tuple-element.4) | copy-start | bytes 1966084
  306.0 9.8 %collective-permute-start.8 = (bf16[128,1024]{1,0:T(8,128)(2,1)S(1)}, bf16[128,1024]{1,0:T(8,128)(2,1)S(1)}, u32[]{:S(2)}, u32[]{:S(2)}) collective-permute-start(bf16[128,1024]{1,0:T(8,128)(2,1)S(1)} %slice.10), channel_id=1, source_target_pairs={{3,0},{7,4},{11,8},{15,12},{19,16},{23,20},{27,24},{31,28}} | collective-permute-start | bytes 786440 | tf_op jit(solution)/shard_map/ppermute | solution.py:235
  307.6 12.9 %collective-permute-start.7 = (bf16[128,512]{1,0:T(8,128)(2,1)S(1)}, bf16[128,512]{1,0:T(8,128)(2,1)S(1)}, u32[]{:S(2)}, u32[]{:S(2)}) collective-permute-start(bf16[128,512]{1,0:T(8,128)(2,1)S(1)} %slice.11), channel_id=1, source_target_pairs={{2,0},{3,1},{6,4},{7,5},{10,8},{11,9},{14,12},{15,13},{18,16},{19,... | collective-permute-start | bytes 393224 | tf_op jit(solution)/shard_map/ppermute | solution.py:234
  309.2 11.3 %slice-start.4 = ((s8[8388608]{0:T(1024)(128)(4,1)}), s8[4194304]{0:T(1024)(128)(4,1)S(1)}, s32[]{:S(2)}) async-start(s8[8388608]{0:T(1024)(128)(4,1)} %bitcast.27), calls=%async_computation.6 | async-start | bytes 8388608
  314.1 6.3 %slice-start.5 = ((s8[8388608]{0:T(1024)(128)(4,1)}), s8[4194304]{0:T(1024)(128)(4,1)S(1)}, s32[]{:S(2)}) async-start(s8[8388608]{0:T(1024)(128)(4,1)} %bitcast.27), calls=%async_computation.7 | async-start | bytes 8388608
  323.1 33.2 %all-to-all-start = ((bf16[128,8,512]{2,0,1:T(8,128)(2,1)}), bf16[128,8,512]{2,0,1:T(8,128)(2,1)S(1)}, u32[]{:S(2)}, u32[]{:S(2)}) async-start(bf16[128,8,512]{2,0,1:T(8,128)(2,1)} %bitcast.21), calls=%async_computation | async-start | bytes 2097152 | tf_op jit(solution)/shard_map/all_to_all | solution.py:248
Sparse Core Ops, SparseCore 0:
  35.8 126.4 all-gather.1
